TPU v7x, 32 devices: a whole 2x2x4 slice. The times are simulated.
32 devices in a mesh: dp: 8 (over y, x, core), expert: 4 (over z).
Axes of the slice: x: 2, y: 2, z: 4, core: 2. Of those that a mesh axis runs over, the one named last changes fastest.
Arguments:
- hidden_in: bfloat16 [16384, 1024], P(('dp', 'expert')), may hold values from -6 to 6
- norm1_gain: bfloat16 [1024], P(('dp', 'expert')), may hold values from 0.5 to 1.5
- w_query: bfloat16 [1024, 1024], P(('dp', 'expert')), may hold values from -0.1875 to 0.1875
- w_key: bfloat16 [1024, 512], P(('dp', 'expert')), may hold values from -0.1875 to 0.1875
- w_value: bfloat16 [1024, 512], P(('dp', 'expert')), may hold values from -0.1875 to 0.1875
- w_out: bfloat16 [1024, 1024], P(('dp', 'expert')), may hold values from -2 to 2
- norm2_gain: bfloat16 [1024], P(('dp', 'expert')), may hold values from 0.5 to 1.5
- w_router: bfloat16 [1024, 32], P(('dp', 'expert')), may hold values from -0.09375 to 0.09375
- w_gate: bfloat16 [32, 1024, 512], P('expert', 'dp'), may hold values from -0.1875 to 0.1875
- w_up: bfloat16 [32, 1024, 512], P('expert', 'dp'), may hold values from -0.1875 to 0.1875
- w_down: bfloat16 [32, 512, 1024], P('expert', None, 'dp'), may hold values from -1 to 1
- expert_ids: int32 [16384, 8], P(('dp', 'expert')), may hold values from 0 to 31, all different within a row; in each aligned block of 512 rows (0 to 511, 512 to 1023, ...) at most 152 rows name the same one
- out_grad: bfloat16 [16384, 1024], P(('dp', 'expert')), may hold values from -6 to 6
Outputs:
- layer_out: bfloat16 [16384, 1024], P(('dp', 'expert'))
- in_grad: bfloat16 [16384, 1024], P(('dp', 'expert'))
- grad_norm1: float32 [1024], P(('dp', 'expert'))
- grad_query: float32 [1024, 1024], P(('dp', 'expert'))
- grad_key: float32 [1024, 512], P(('dp', 'expert'))
- grad_value: float32 [1024, 512], P(('dp', 'expert'))
- grad_out: float32 [1024, 1024], P(('dp', 'expert'))
- grad_norm2: float32 [1024], P(('dp', 'expert'))
- grad_router: float32 [1024, 32], P(('dp', 'expert'))
- grad_gate: float32 [32, 1024, 512], P('expert', 'dp')
- grad_up: float32 [32, 1024, 512], P('expert', 'dp')
- grad_down: float32 [32, 512, 1024], P('expert', None, 'dp')
Inputs may be any that keep to these rules, and one draw needn't show every extreme that they name: `expert_ids`: each row names 8 different experts; among the 512 rows of one device no expert is named more than 152 times, a bound that some block reaches.
All inputs are finite; a program needn't handle non-finite values.
Results may differ from a plain program's by a relative error of at most 0.015.
Values may be sent and summed in bfloat16 or wider, within the bound.
A program may use at most 256 MiB of HBM per device.

v0:
```python
import math

import jax
import jax.numpy as jnp
from jax import lax
from jax.sharding import PartitionSpec as P

HEADS = 16
KV_HEADS = 8
HEAD_DIM = 64
EXPERTS = 32
TOPK = 8
CAP = 152


EPSILON = 1e-06


def rope_tables(length, head_width):
    half_width = head_width // 2
    ladder = jnp.arange(half_width, dtype=jnp.float32) * (2.0 / head_width)
    inverse = jnp.exp(-math.log(10000.0) * ladder)
    angles = jnp.arange(length, dtype=jnp.float32)[:, None] * inverse[None, :]
    return (jnp.cos(angles), jnp.sin(angles))


def rotate(values, cosine, sine_table):
    half_width = values.shape[-1] // 2
    first_half = values[..., :half_width]
    second = values[..., half_width:]
    cos_rows = cosine[:, None, :]
    sin_rows = sine_table[:, None, :]
    return jnp.concatenate(
        [first_half * cos_rows - second * sin_rows, second * cos_rows + first_half * sin_rows],
        axis=-1,
    )


def unrotate(grads, cosine, sine_table):
    half_width = grads.shape[-1] // 2
    first_half = grads[..., :half_width]
    second = grads[..., half_width:]
    cos_rows = cosine[:, None, :]
    sin_rows = sine_table[:, None, :]
    return jnp.concatenate(
        [first_half * cos_rows + second * sin_rows, second * cos_rows - first_half * sin_rows],
        axis=-1,
    )


def slot_table(routes):
    flat_ids = routes.reshape(-1)
    row_count = flat_ids.shape[0]
    hit_table = (flat_ids[:, None] == jnp.arange(EXPERTS, dtype=jnp.int32)[None, :]).astype(
        jnp.int32
    )
    before = jnp.cumsum(hit_table, axis=0) - hit_table
    slot_rank = jnp.sum(before * hit_table, axis=1)
    position = flat_ids * CAP + slot_rank
    table = (
        jnp.full((EXPERTS * CAP,), row_count, jnp.int32)
        .at[position]
        .set(jnp.arange(row_count, dtype=jnp.int32))
    )
    return (position, table)


def block_scores(query_block, keys, start, scale):
    scores = (
        jnp.einsum("qgrd,kgd->grqk", query_block, keys, preferred_element_type=jnp.float32) * scale
    )
    query_pos = start + jnp.arange(query_block.shape[0], dtype=jnp.int32)
    key_pos = jnp.arange(keys.shape[0], dtype=jnp.int32)
    return jnp.where(key_pos[None, :] <= query_pos[:, None], scores, -1e30)


def local(
    hidden_in,
    norm1_gain,
    w_query,
    w_key,
    w_value,
    w_out,
    norm2_gain,
    w_router,
    w_gate,
    w_up,
    w_down,
    expert_ids,
    out_grad,
):
    gain_one, query_w, key_w, value_w, out_w, gain_two, router_w = (
        lax.all_gather(norm1_gain, ("dp", "expert"), axis=0, tiled=True),
        lax.all_gather(w_query, ("dp", "expert"), axis=0, tiled=True),
        lax.all_gather(w_key, ("dp", "expert"), axis=0, tiled=True),
        lax.all_gather(w_value, ("dp", "expert"), axis=0, tiled=True),
        lax.all_gather(w_out, ("dp", "expert"), axis=0, tiled=True),
        lax.all_gather(norm2_gain, ("dp", "expert"), axis=0, tiled=True),
        lax.all_gather(w_router, ("dp", "expert"), axis=0, tiled=True),
    )
    gate_w, up_w, down_w = (
        lax.all_gather(w_gate, "dp", axis=1, tiled=True),
        lax.all_gather(w_up, "dp", axis=1, tiled=True),
        lax.all_gather(w_down, "dp", axis=2, tiled=True),
    )
    owners = lax.axis_size("expert")
    local_experts = EXPERTS // owners
    inputs = hidden_in.astype(jnp.float32)
    length = inputs.shape[0]
    width = inputs.shape[1]
    group = HEADS // KV_HEADS
    scale = 1.0 / math.sqrt(HEAD_DIM)
    block_rows = min(512, length)
    cosine, sine_table = rope_tables(length, HEAD_DIM)
    factor_one = lax.rsqrt(jnp.mean(inputs * inputs, axis=-1, keepdims=True) + EPSILON)
    scaled_one = inputs * factor_one
    normed = (scaled_one * gain_one.astype(jnp.float32)).astype(jnp.bfloat16)
    queries = jnp.dot(normed, query_w, preferred_element_type=jnp.float32).reshape(
        length, HEADS, HEAD_DIM
    )
    keys = jnp.dot(normed, key_w, preferred_element_type=jnp.float32).reshape(
        length, KV_HEADS, HEAD_DIM
    )
    values_in = (
        jnp.dot(normed, value_w, preferred_element_type=jnp.float32)
        .astype(jnp.bfloat16)
        .reshape(length, KV_HEADS, HEAD_DIM)
    )
    queries = (
        rotate(queries, cosine, sine_table)
        .astype(jnp.bfloat16)
        .reshape(length, KV_HEADS, group, HEAD_DIM)
    )
    keys = rotate(keys, cosine, sine_table).astype(jnp.bfloat16)
    block_index = 0
    start = block_index * block_rows
    scores = block_scores(queries, keys, start, scale)
    top_score = jnp.max(scores, axis=-1, keepdims=True)
    log_total = top_score + jnp.log(jnp.sum(jnp.exp(scores - top_score), axis=-1, keepdims=True))
    weights = jnp.exp(scores - log_total).astype(jnp.bfloat16)
    pieces = jnp.einsum("grqk,kgd->qgrd", weights, values_in, preferred_element_type=jnp.float32)
    log_totals = [log_total]
    attended = pieces.reshape(length, HEADS * HEAD_DIM).astype(jnp.bfloat16)
    middle = inputs + jnp.dot(attended, out_w, preferred_element_type=jnp.float32)
    factor_two = lax.rsqrt(jnp.mean(middle * middle, axis=-1, keepdims=True) + EPSILON)
    scaled_two = middle * factor_two
    gain_float = gain_two.astype(jnp.float32)
    normed_two = (scaled_two * gain_float).astype(jnp.bfloat16)
    logits = jnp.dot(normed_two, router_w, preferred_element_type=jnp.float32)
    hit_table = (
        expert_ids[:, :, None] == jnp.arange(EXPERTS, dtype=jnp.int32)[None, None, :]
    ).astype(jnp.float32)
    picked = jnp.sum(hit_table * logits[:, None, :], axis=-1)
    gates = jax.nn.softmax(picked, axis=-1)
    position, table = slot_table(expert_ids)
    padded = jnp.concatenate([normed_two, jnp.zeros((1, width), jnp.bfloat16)], axis=0)
    outgoing = padded[table // TOPK].reshape(owners, local_experts, CAP, width)
    rows = lax.all_to_all(outgoing, "expert", split_axis=0, concat_axis=0, tiled=True)
    gate_pre = jnp.einsum("sjcd,jdf->sjcf", rows, gate_w, preferred_element_type=jnp.float32)
    up_pre = jnp.einsum("sjcd,jdf->sjcf", rows, up_w, preferred_element_type=jnp.float32)
    hidden = (jax.nn.silu(gate_pre) * up_pre).astype(jnp.bfloat16)
    result = jnp.einsum(
        "sjcf,jfd->sjcd", hidden, down_w, preferred_element_type=jnp.float32
    ).astype(jnp.bfloat16)
    result, gate_pre, up_pre = (result, gate_pre, up_pre)
    coming_back = lax.all_to_all(result, "expert", split_axis=0, concat_axis=0, tiled=True)
    coming_back, rows, gate_pre, up_pre = (coming_back, rows, gate_pre, up_pre)
    per_choice = (
        coming_back.reshape(EXPERTS * CAP, width)[position]
        .reshape(length, TOPK, width)
        .astype(jnp.float32)
    )
    mixed = jnp.sum(gates[:, :, None] * per_choice, axis=1)
    layer_out = (middle + mixed).astype(jnp.bfloat16)
    upstream = out_grad.astype(jnp.float32)
    choice_grads = (gates[:, :, None] * upstream[:, None, :]).astype(jnp.bfloat16)
    gate_grads = jnp.sum(upstream[:, None, :] * per_choice, axis=-1)
    picked_grads = gates * (gate_grads - jnp.sum(gates * gate_grads, axis=-1, keepdims=True))
    logit_grads = jnp.sum(hit_table * picked_grads[:, :, None], axis=1).astype(jnp.bfloat16)
    router_grad = jnp.einsum(
        "td,te->de", normed_two, logit_grads, preferred_element_type=jnp.float32
    )
    normed_grad = jnp.einsum("te,de->td", logit_grads, router_w, preferred_element_type=jnp.float32)
    grad_rows = jnp.concatenate(
        [choice_grads.reshape(length * TOPK, width), jnp.zeros((1, width), jnp.bfloat16)], axis=0
    )
    grad_outgoing = grad_rows[table].reshape(owners, local_experts, CAP, width)
    arrived = lax.all_to_all(grad_outgoing, "expert", split_axis=0, concat_axis=0, tiled=True)
    gate_back, up_back, down_back = (
        lax.all_gather(w_gate, "dp", axis=1, tiled=True),
        lax.all_gather(w_up, "dp", axis=1, tiled=True),
        lax.all_gather(w_down, "dp", axis=2, tiled=True),
    )
    sigmoid_gate = jax.nn.sigmoid(gate_pre)
    activated = jax.nn.silu(gate_pre)
    hidden = (activated * up_pre).astype(jnp.bfloat16)
    down_grad = jnp.einsum("sjcf,sjcd->jfd", hidden, arrived, preferred_element_type=jnp.float32)
    hidden_grad = jnp.einsum(
        "sjcd,jfd->sjcf", arrived, down_back, preferred_element_type=jnp.float32
    )
    gate_pre_grad = (
        hidden_grad * up_pre * sigmoid_gate * (1.0 + gate_pre * (1.0 - sigmoid_gate))
    ).astype(jnp.bfloat16)
    up_pre_grad = (hidden_grad * activated).astype(jnp.bfloat16)
    gate_grad = jnp.einsum(
        "sjcd,sjcf->jdf", rows, gate_pre_grad, preferred_element_type=jnp.float32
    )
    up_grad = jnp.einsum("sjcd,sjcf->jdf", rows, up_pre_grad, preferred_element_type=jnp.float32)
    row_grads = jnp.einsum(
        "sjcf,jdf->sjcd", gate_pre_grad, gate_back, preferred_element_type=jnp.float32
    )
    row_grads = (
        row_grads
        + jnp.einsum("sjcf,jdf->sjcd", up_pre_grad, up_back, preferred_element_type=jnp.float32)
    ).astype(jnp.bfloat16)
    sent_back = lax.all_to_all(row_grads, "expert", split_axis=0, concat_axis=0, tiled=True)
    gate_total, up_total, down_total = (
        lax.psum_scatter(
            gate_grad.astype(jnp.bfloat16), "dp", scatter_dimension=1, tiled=True
        ).astype(jnp.float32),
        lax.psum_scatter(
            up_grad.astype(jnp.bfloat16), "dp", scatter_dimension=1, tiled=True
        ).astype(jnp.float32),
        lax.psum_scatter(
            down_grad.astype(jnp.bfloat16), "dp", scatter_dimension=2, tiled=True
        ).astype(jnp.float32),
    )
    returned_rows = (
        sent_back.reshape(EXPERTS * CAP, width)[position]
        .reshape(length, TOPK, width)
        .astype(jnp.float32)
    )
    normed_grad = normed_grad + jnp.sum(returned_rows, axis=1)
    gain_two_grad = jnp.sum(normed_grad * scaled_two, axis=0)
    scaled_grad = normed_grad * gain_float
    middle_grad = upstream + factor_two * (
        scaled_grad - scaled_two * jnp.mean(scaled_grad * scaled_two, axis=-1, keepdims=True)
    )
    branch_grad = middle_grad.astype(jnp.bfloat16)
    out_w_grad = jnp.einsum("tk,td->kd", attended, branch_grad, preferred_element_type=jnp.float32)
    attended_grad = jnp.einsum(
        "td,kd->tk", branch_grad, out_w, preferred_element_type=jnp.float32
    ).astype(jnp.bfloat16)
    attended_grad = attended_grad.reshape(length, KV_HEADS, group, HEAD_DIM)
    key_grads = jnp.zeros((length, KV_HEADS, HEAD_DIM), jnp.float32)
    value_grads = jnp.zeros((length, KV_HEADS, HEAD_DIM), jnp.float32)
    block_index = 0
    start = block_index * block_rows
    key_len = start + block_rows
    scores = block_scores(queries, keys, start, scale)
    weights = jnp.exp(scores - log_totals[block_index])
    value_grads = value_grads.at[:key_len].add(
        jnp.einsum(
            "grqk,qgrd->kgd",
            weights.astype(jnp.bfloat16),
            attended_grad,
            preferred_element_type=jnp.float32,
        )
    )
    weight_grads = jnp.einsum(
        "qgrd,kgd->grqk", attended_grad, values_in, preferred_element_type=jnp.float32
    )
    centre = jnp.sum(weights * weight_grads, axis=-1, keepdims=True)
    score_grads = (weights * (weight_grads - centre)).astype(jnp.bfloat16)
    query_pieces = (
        jnp.einsum("grqk,kgd->qgrd", score_grads, keys, preferred_element_type=jnp.float32) * scale
    )
    key_grads = key_grads.at[:key_len].add(
        jnp.einsum("grqk,qgrd->kgd", score_grads, queries, preferred_element_type=jnp.float32)
        * scale
    )
    query_grads = query_pieces.reshape(length, HEADS, HEAD_DIM)
    query_grads = (
        unrotate(query_grads, cosine, sine_table)
        .reshape(length, HEADS * HEAD_DIM)
        .astype(jnp.bfloat16)
    )
    key_grads = (
        unrotate(key_grads, cosine, sine_table)
        .reshape(length, KV_HEADS * HEAD_DIM)
        .astype(jnp.bfloat16)
    )
    value_grads = value_grads.reshape(length, KV_HEADS * HEAD_DIM).astype(jnp.bfloat16)
    query_w_grad = jnp.einsum("td,tk->dk", normed, query_grads, preferred_element_type=jnp.float32)
    key_w_grad = jnp.einsum("td,tk->dk", normed, key_grads, preferred_element_type=jnp.float32)
    value_w_grad = jnp.einsum("td,tk->dk", normed, value_grads, preferred_element_type=jnp.float32)
    first_grad = jnp.einsum("tk,dk->td", query_grads, query_w, preferred_element_type=jnp.float32)
    first_grad = first_grad + jnp.einsum(
        "tk,dk->td", key_grads, key_w, preferred_element_type=jnp.float32
    )
    first_grad = first_grad + jnp.einsum(
        "tk,dk->td", value_grads, value_w, preferred_element_type=jnp.float32
    )
    gain_one_grad = jnp.sum(first_grad * scaled_one, axis=0)
    scaled_one_grad = first_grad * gain_one.astype(jnp.float32)
    input_grad = middle_grad + factor_one * (
        scaled_one_grad
        - scaled_one * jnp.mean(scaled_one_grad * scaled_one, axis=-1, keepdims=True)
    )
    sums = (
        lax.psum_scatter(gain_one_grad, ("dp", "expert"), scatter_dimension=0, tiled=True),
        lax.psum_scatter(query_w_grad, ("dp", "expert"), scatter_dimension=0, tiled=True),
        lax.psum_scatter(key_w_grad, ("dp", "expert"), scatter_dimension=0, tiled=True),
        lax.psum_scatter(value_w_grad, ("dp", "expert"), scatter_dimension=0, tiled=True),
        lax.psum_scatter(out_w_grad, ("dp", "expert"), scatter_dimension=0, tiled=True),
        lax.psum_scatter(gain_two_grad, ("dp", "expert"), scatter_dimension=0, tiled=True),
        lax.psum_scatter(router_grad, ("dp", "expert"), scatter_dimension=0, tiled=True),
    )
    return (
        layer_out,
        input_grad.astype(jnp.bfloat16),
        sums[0],
        sums[1],
        sums[2],
        sums[3],
        sums[4],
        sums[5],
        sums[6],
        gate_total,
        up_total,
        down_total,
    )


def solution(mesh):
    return jax.shard_map(
        local,
        mesh=mesh,
        in_specs=(
            P(("dp", "expert"), None),
            P(("dp", "expert")),
            P(("dp", "expert"), None),
            P(("dp", "expert"), None),
            P(("dp", "expert"), None),
            P(("dp", "expert"), None),
            P(("dp", "expert")),
            P(("dp", "expert"), None),
            P("expert", "dp", None),
            P("expert", "dp", None),
            P("expert", None, "dp"),
            P(("dp", "expert"), None),
            P(("dp", "expert"), None),
        ),
        out_specs=(
            P(("dp", "expert"), None),
            P(("dp", "expert"), None),
            P(("dp", "expert")),
            P(("dp", "expert"), None),
            P(("dp", "expert"), None),
            P(("dp", "expert"), None),
            P(("dp", "expert"), None),
            P(("dp", "expert")),
            P(("dp", "expert"), None),
            P("expert", "dp", None),
            P("expert", "dp", None),
            P("expert", None, "dp"),
        ),
        check_vma=False,
    )
```

profile of v0, /device:TPU:0, one launch (start us, length us, event | category | flops | bytes accessed | tf_op | source)
XLA Modules:
  0.0 2124.1 jit_solution(17505956882476982829)
XLA Ops:
  13.4 42.1 %all-reduce.7 = (bf16[1024]{0:T(1024)(128)(2,1)S(1)}, bf16[1024]{0:T(1024)(128)(2,1)S(1)}) all-reduce(bf16[1024]{0:T(1024)(128)(2,1)S(1)} %dynamic-update-slice.4, bf16[1024]{0:T(1024)(128)(2,1)S(1)} %dynamic-update-slice.5), channel_id=1, replica_groups=mesh['dp'=8,'expert'=4] {'dp','expert'}, use_global_device_ids=true, to_apply=%add.2 | all-reduce | flops 2048 | bytes 8192
  67.5 15.5 scatter_custom_fusion
  86.7 36.7 %all-gather.8.cloned.1.call-done = bf16[1024,512]{1,0:T(8,128)(2,1)} async-done(((bf16[32,512]{1,0:T(8,128)(2,1)}), bf16[1024,512]{1,0:T(8,128)(2,1)}) %all-gather.8.cloned.1.call-update) | async-done | bytes 1048592 | tf_op jit(solution)/shard_map/all_gather | solution.py:96
  125.5 56.3 %all-gather.12.cloned.1.call-done = bf16[1024,1024]{1,0:T(8,128)(2,1)} async-done(((bf16[32,1024]{1,0:T(8,128)(2,1)}), bf16[1024,1024]{1,0:T(8,128)(2,1)}) %all-gather.12.cloned.1.call-update) | async-done | bytes 2097168 | tf_op jit(solution)/shard_map/all_gather | solution.py:94
  210.2 29.8 %all-gather.14.cloned.1.call-done = bf16[1024,1024]{1,0:T(8,128)(2,1)} async-done(((bf16[32,1024]{1,0:T(8,128)(2,1)}), bf16[1024,1024]{1,0:T(8,128)(2,1)}) %all-gather.14.cloned.1.call-update) | async-done | bytes 2097168 | tf_op jit(solution)/shard_map/all_gather | solution.py:97
  244.6 15.7 gather_fusion
  268.4 274.7 %all_gather.39 = bf16[1024,32]{1,0:T(8,128)(2,1)S(1)} all-gather(bf16[32,32]{1,0:T(8,128)(2,1)S(1)} %copy-done.60), channel_id=1, replica_groups=mesh['dp'=8,'expert'=4] {'dp','expert'}, dimensions={0}, use_global_device_ids=true | all-gather | bytes 67584 | tf_op jit(solution)/shard_map/all_gather | solution.py:99
  557.1 26.2 %gather_fusion.2 = bf16[4864,1024]{1,0:T(8,128)(2,1)} fusion(bf16[4097,1024]{1,0:T(8,128)(2,1)} %concatenate.36, s32[5120]{0:T(1024)S(1)} %copy-done.46), kind=kCustom, calls=%fused_computation.2 | custom fusion | bytes 19942400 | tf_op jit(solution)/shard_map/gather | solution.py:187
  590.0 13.0 fusion.21
  603.1 12.6 fusion.23
  615.7 32.7 %all-gather.20.cloned.1.call-done = bf16[8,512,1024]{2,1,0:T(8,128)(2,1)} async-done(((bf16[8,512,128]{2,1,0:T(8,128)(2,1)}), bf16[8,512,1024]{2,1,0:T(8,128)(2,1)}) %all-gather.20.cloned.1.call-update) | async-done | bytes 8388624 | tf_op jit(solution)/shard_map/all_gather | solution.py:104
  648.4 153.2 %all-to-all-done.2 = bf16[4,8,152,1024]{3,2,1,0:T(8,128)(2,1)} async-done(((bf16[4,8,152,1024]{3,2,1,0:T(8,128)(2,1)}), bf16[4,8,152,1024]{3,2,1,0:T(8,128)(2,1)}, u32[]{:S(2)}, u32[]{:S(2)}) %all-to-all-start.2) | async-done | bytes 9961504 | tf_op jit(solution)/shard_map/all_to_all | solution.py:188
  801.5 22.5 %fusion.10 = (bf16[4,8,152,512]{3,2,0,1:T(8,128)(2,1)}, bf16[4,8,152,512]{3,2,0,1:T(8,128)(2,1)}, bf16[4,8,152,512]{3,2,0,1:T(8,128)(2,1)}) fusion(f32[8,4,152,512]{3,2,1,0:T(8,128)} %fusion.21, f32[8,4,152,512]{3,2,1,0:T(8,128)} %fusion.23, bf16[8,512,1024]{2,1,0:T(8,128)(2,1)} %all-gather.20.cloned.1.call-done, bf16[4,8,152,1024]{3,2,1,0:T(8,128)(2,1)} %all-to-all-done.2), kind=kOutput, calls=%fused_computation.30 | convolution fusion | flops 5137629184 | bytes 53215232 | tf_op jit(solution)/shard_map/sjcd,jfd->sjcf/dot_general | solution.py:198
  824.0 13.6 bitcast_convert_fusion
  837.6 12.8 copy.126
  850.5 12.3 copy.129
  862.8 12.7 convert_bitcast_fusion
  891.2 13.4 bitcast_convert_fusion.2
  904.6 14.1 fusion.25
  918.7 17.6 fusion.7
  946.5 161.3 %all-to-all-done.1 = bf16[4,8,152,1024]{3,2,1,0:T(8,128)(2,1)} async-done(((bf16[4,8,152,1024]{3,2,1,0:T(8,128)(2,1)}), bf16[4,8,152,1024]{3,2,1,0:T(8,128)(2,1)}, u32[]{:S(2)}, u32[]{:S(2)}) %all-to-all-start.1) | async-done | bytes 9961504 | tf_op jit(solution)/shard_map/all_to_all | solution.py:166
  1113.7 13.2 bitcast_convert_fusion.1
  1127.7 26.1 %gather_fusion.1 = bf16[4096,1024]{1,0:T(8,128)(2,1)} fusion(bf16[4864,1024]{1,0:T(8,128)(2,1)} %bitcast.25, s32[4096]{0:T(1024)S(1)} %broadcast_clamp_fusion), kind=kCustom, calls=%fused_computation.1 | custom fusion | bytes 16793600 | tf_op jit(solution)/shard_map/gather | solution.py:169
  1163.8 166.1 %all-to-all-done.3 = bf16[4,8,152,1024]{3,2,1,0:T(8,128)(2,1)} async-done(((bf16[4,8,152,1024]{3,2,1,0:T(8,128)(2,1)}), bf16[4,8,152,1024]{3,2,1,0:T(8,128)(2,1)}, u32[]{:S(2)}, u32[]{:S(2)}) %all-to-all-start.3) | async-done | bytes 9961504 | tf_op jit(solution)/shard_map/all_to_all | solution.py:216
  1330.0 26.2 %gather_fusion.3 = bf16[4096,1024]{1,0:T(8,128)(2,1)} fusion(bf16[4864,1024]{1,0:T(8,128)(2,1)} %bitcast.35, s32[4096]{0:T(1024)S(1)} %broadcast_clamp_fusion), kind=kCustom, calls=%fused_computation.3 | custom fusion | bytes 16793600 | tf_op jit(solution)/shard_map/gather | solution.py:229
  1376.0 15.3 fusion.2
  1459.0 37.0 %all-reduce.6 = (f32[1024]{0:T(1024)S(1)}, f32[1024]{0:T(1024)S(1)}) all-reduce(f32[1024]{0:T(1024)S(1)} %get-tuple-element.56, f32[1024]{0:T(1024)S(1)} %get-tuple-element.54), channel_id=2, replica_groups=mesh['dp'=8,'expert'=4] {'dp','expert'}, use_global_device_ids=true, to_apply=%region_20.21.clone | all-reduce | flops 2048 | bytes 16384
  1500.3 42.8 %reduce-scatter.19.cloned.1.call-done = f32[32,32]{1,0:T(8,128)} async-done(((f32[1024,32]{1,0:T(8,128)}), f32[32,32]{1,0:T(8,128)}) %reduce-scatter.19.cloned.1.call-update) | async-done | bytes 4112 | tf_op jit(solution)/shard_map/reduce_scatter | solution.py:307
  1543.2 137.0 %reduce-scatter.13.cloned.1.call-done = f32[32,512]{1,0:T(8,128)} async-done(((f32[1024,512]{1,0:T(8,128)}), f32[32,512]{1,0:T(8,128)}) %reduce-scatter.13.cloned.1.call-update) | async-done | bytes 65552 | tf_op jit(solution)/shard_map/reduce_scatter | solution.py:303
  1680.1 139.0 %reduce-scatter.15.cloned.1.call-done = f32[32,512]{1,0:T(8,128)} async-done(((f32[1024,512]{1,0:T(8,128)}), f32[32,512]{1,0:T(8,128)}) %reduce-scatter.15.cloned.1.call-update) | async-done | bytes 65552 | tf_op jit(solution)/shard_map/reduce_scatter | solution.py:304
  1819.2 148.7 %reduce-scatter.11.cloned.1.call-done = f32[32,1024]{1,0:T(8,128)} async-done(((f32[1024,1024]{1,0:T(8,128)}), f32[32,1024]{1,0:T(8,128)}) %reduce-scatter.11.cloned.1.call-update) | async-done | bytes 131088 | tf_op jit(solution)/shard_map/reduce_scatter | solution.py:302
  1967.9 149.2 %reduce-scatter.17.cloned.1.call-done = f32[32,1024]{1,0:T(8,128)} async-done(((f32[1024,1024]{1,0:T(8,128)}), f32[32,1024]{1,0:T(8,128)}) %reduce-scatter.17.cloned.1.call-update) | async-done | bytes 131088 | tf_op jit(solution)/shard_map/reduce_scatter | solution.py:305
  (263 shorter events, 219.0 us)
Async XLA Ops:
  7.2 76.6 %copy-start = (bf16[512,1024]{1,0:T(8,128)(2,1)S(1)}, bf16[512,1024]{1,0:T(8,128)(2,1)}, u32[]{:S(2)}) copy-start(bf16[512,1024]{1,0:T(8,128)(2,1)} %param.21) | copy-start | bytes 3145732
  7.2 77.3 %all-gather.10.cloned.1.call-start = ((), (), s32[]{:S(2)}) async-start(), calls=%async_computation.13 | async-start | bytes 1081344 | tf_op jit(solution)/shard_map/all_gather | solution.py:95
  7.9 115.5 %all-gather.8.cloned.1.call-start = ((), (), s32[]{:S(2)}) async-start(), calls=%async_computation.12 | async-start | bytes 1081344 | tf_op jit(solution)/shard_map/all_gather | solution.py:96
  8.7 173.2 %all-gather.12.cloned.1.call-start = ((), (), s32[]{:S(2)}) async-start(), calls=%async_computation.14 | async-start | bytes 2162688 | tf_op jit(solution)/shard_map/all_gather | solution.py:94
  9.4 230.6 %all-gather.14.cloned.1.call-start = ((), (), s32[]{:S(2)}) async-start(), calls=%async_computation.15 | async-start | bytes 2162688 | tf_op jit(solution)/shard_map/all_gather | solution.py:97
  10.0 580.0 %all-gather.18.cloned.1.call-start = ((), (), s32[]{:S(2)}) async-start(), calls=%async_computation.17 | async-start | bytes 9437184 | tf_op jit(solution)/shard_map/all_gather | solution.py:103
  55.5 126.3 %copy-start.44 = (f32[1024]{0:T(1024)}, f32[1024]{0:T(1024)S(1)}, u32[]{:S(2)}) copy-start(f32[1024]{0:T(1024)S(1)} %convert_element_type.142) | copy-start | bytes 12292
  55.5 187.5 %copy-start.50 = (f32[1024]{0:T(1024)}, f32[1024]{0:T(1024)S(1)}, u32[]{:S(2)}) copy-start(f32[1024]{0:T(1024)S(1)} %convert_element_type.149) | copy-start | bytes 12292
  84.1 100.7 %copy-start.52 = (f32[512]{0:T(512)}, f32[512]{0:T(512)S(1)}, u32[]{:S(2)}) copy-start(f32[512]{0:T(512)S(1)} %add_rsqrt_fusion.1) | copy-start | bytes 6148
  84.4 100.4 %copy-start.27 = (f32[512,32]{0,1:T(8,128)}, f32[512,32]{0,1:T(8,128)S(1)}, u32[]{:S(2)}) copy-start(f32[512,32]{0,1:T(8,128)S(1)} %get-tuple-element.77) | copy-start | bytes 196612
  84.4 100.4 %copy-start.29 = (f32[512,32]{0,1:T(8,128)}, f32[512,32]{0,1:T(8,128)S(1)}, u32[]{:S(2)}) copy-start(f32[512,32]{0,1:T(8,128)S(1)} %get-tuple-element.78) | copy-start | bytes 196612
  86.7 98.5 %copy-start.34 = (bf16[512,8,32]{0,2,1:T(8,128)(2,1)}, bf16[512,8,32]{0,2,1:T(8,128)(2,1)S(1)}, u32[]{:S(2)}) copy-start(bf16[512,8,32]{0,2,1:T(8,128)(2,1)S(1)} %get-tuple-element.73) | copy-start | bytes 786436
  86.7 98.5 %copy-start.36 = (bf16[512,8,32]{0,2,1:T(8,128)(2,1)}, bf16[512,8,32]{0,2,1:T(8,128)(2,1)S(1)}, u32[]{:S(2)}) copy-start(bf16[512,8,32]{0,2,1:T(8,128)(2,1)S(1)} %get-tuple-element.74) | copy-start | bytes 786436
  125.5 75.6 %copy-start.20 = (bf16[512,512]{0,1:T(8,128)(2,1)}, bf16[512,512]{0,1:T(8,128)(2,1)S(1)}, u32[]{:S(2)}) copy-start(bf16[512,512]{0,1:T(8,128)(2,1)S(1)} %convolution_convert_fusion.1) | copy-start | bytes 1572868
  210.2 32.8 %copy-start.10 = (bf16[8,64,2,512]{3,1,2,0:T(8,128)(2,1)}, bf16[8,64,2,512]{3,1,2,0:T(8,128)(2,1)S(1)}, u32[]{:S(2)}) copy-start(bf16[8,64,2,512]{3,1,2,0:T(8,128)(2,1)S(1)} %fusion.58) | copy-start | bytes 3145732
  244.5 298.6 %copy-start.8 = (bf16[512,1024]{1,0:T(8,128)(2,1)}, bf16[512,1024]{1,0:T(8,128)(2,1)S(1)}, u32[]{:S(2)}) copy-start(bf16[512,1024]{1,0:T(8,128)(2,1)S(1)} %multiply_convert_fusion) | copy-start | bytes 3145732
  260.3 323.0 %all-to-all-start = ((bf16[4,8,152,1024]{3,2,1,0:T(8,128)(2,1)}), bf16[4,8,152,1024]{3,2,1,0:T(8,128)(2,1)}, u32[]{:S(2)}, u32[]{:S(2)}) async-start(bf16[4,8,152,1024]{3,2,1,0:T(8,128)(2,1)} %bitcast.211), calls=%async_computation | async-start | bytes 19922944 | tf_op jit(solution)/shard_map/all_to_all | solution.py:158
  266.3 277.4 %copy-start.42 = (s32[512,8]{0,1:T(8,128)S(1)}, s32[512,8]{0,1:T(8,128)}, u32[]{:S(2)}) copy-start(s32[512,8]{0,1:T(8,128)} %param.32) | copy-start | bytes 49156
  266.3 336.7 %all-gather.16.cloned.1.call-start = ((), (), s32[]{:S(2)}) async-start(), calls=%async_computation.16 | async-start | bytes 9437184 | tf_op jit(solution)/shard_map/all_gather | solution.py:102
  268.4 280.9 %copy-start.4 = (f32[512,1024]{1,0:T(8,128)}, f32[512,1024]{1,0:T(8,128)S(1)}, u32[]{:S(2)}) copy-start(f32[512,1024]{1,0:T(8,128)S(1)} %convert_element_type.159) | copy-start | bytes 6291460
  583.3 218.2 %all-to-all-start.2 = ((bf16[4,8,152,1024]{3,2,1,0:T(8,128)(2,1)}), bf16[4,8,152,1024]{3,2,1,0:T(8,128)(2,1)}, u32[]{:S(2)}, u32[]{:S(2)}) async-start(bf16[4,8,152,1024]{3,2,1,0:T(8,128)(2,1)} %bitcast.212), calls=%async_computation.2 | async-start | bytes 19922944 | tf_op jit(solution)/shard_map/all_to_all | solution.py:188
  589.2 59.2 %all-gather.20.cloned.1.call-start = ((), (), s32[]{:S(2)}) async-start(), calls=%async_computation.18 | async-start | bytes 9437184 | tf_op jit(solution)/shard_map/all_gather | solution.py:104
  590.0 849.1 %reduce-scatter.25.cloned.1.call-start = ((), (), s32[]{:S(2)}) async-start(), calls=%async_computation.26 | async-start | bytes 9437184
  885.3 222.5 %all-to-all-start.1 = ((bf16[4,8,152,1024]{3,2,1,0:T(8,128)(2,1)}), bf16[4,8,152,1024]{3,2,1,0:T(8,128)(2,1)}, u32[]{:S(2)}, u32[]{:S(2)}) async-start(bf16[4,8,152,1024]{3,2,1,0:T(8,128)(2,1)} %copy.100), calls=%async_computation.1 | async-start | bytes 19922944 | tf_op jit(solution)/shard_map/all_to_all | solution.py:166
  891.1 555.9 %reduce-scatter.21.cloned.1.call-start = ((), (), s32[]{:S(2)}) async-start(), calls=%async_computation.24 | async-start | bytes 9437184 | tf_op jit(solution)/shard_map/reduce_scatter | solution.py:218
  1107.8 222.2 %all-to-all-start.3 = ((bf16[4,8,152,1024]{3,2,1,0:T(8,128)(2,1)}), bf16[4,8,152,1024]{3,2,1,0:T(8,128)(2,1)}, u32[]{:S(2)}, u32[]{:S(2)}) async-start(bf16[4,8,152,1024]{3,2,1,0:T(8,128)(2,1)} %copy.105), calls=%async_computation.3 | async-start | bytes 19922944 | tf_op jit(solution)/shard_map/all_to_all | solution.py:216
  1113.7 336.2 %reduce-scatter.23.cloned.1.call-start = ((), (), s32[]{:S(2)}) async-start(), calls=%async_computation.25 | async-start | bytes 9437184 | tf_op jit(solution)/shard_map/reduce_scatter | solution.py:221
  1127.0 416.2 %reduce-scatter.19.cloned.1.call-start = ((), (), s32[]{:S(2)}) async-start(), calls=%async_computation.23 | async-start | bytes 540672 | tf_op jit(solution)/shard_map/reduce_scatter | solution.py:307
  1410.3 269.8 %reduce-scatter.13.cloned.1.call-start = ((), (), s32[]{:S(2)}) async-start(), calls=%async_computation.20 | async-start | bytes 2162688 | tf_op jit(solution)/shard_map/reduce_scatter | solution.py:303
  1412.7 406.5 %reduce-scatter.15.cloned.1.call-start = ((), (), s32[]{:S(2)}) async-start(), calls=%async_computation.21 | async-start | bytes 2162688 | tf_op jit(solution)/shard_map/reduce_scatter | solution.py:304
  1424.3 543.6 %reduce-scatter.11.cloned.1.call-start = ((), (), s32[]{:S(2)}) async-start(), calls=%async_computation.19 | async-start | bytes 4325376 | tf_op jit(solution)/shard_map/reduce_scatter | solution.py:302
  1434.2 682.9 %reduce-scatter.17.cloned.1.call-start = ((), (), s32[]{:S(2)}) async-start(), calls=%async_computation.22 | async-start | bytes 4325376 | tf_op jit(solution)/shard_map/reduce_scatter | solution.py:305
  (53 other events, 455.6 us)
Sparse Core Ops, SparseCore 0:
  11.0 56.5 all-gather.9
  70.6 52.7 all-gather.7
  126.3 55.4 all-gather.11
  184.6 55.3 all-gather.13
  241.7 53.2 all-gather.17
  296.8 54.3 all-gather.15
  591.9 56.3 all-gather.19
  863.0 69.4 reduce-scatter.24
  936.3 71.2 reduce-scatter.20
  1127.1 71.8 reduce-scatter.22
  1410.5 132.6 reduce-scatter.18
  1545.9 134.2 reduce-scatter.12
  1683.1 136.0 reduce-scatter.14
  1821.9 145.9 reduce-scatter.10
  1970.6 146.4 reduce-scatter.16
where the time goes:
time: 2130 us; the launch traced here: 2120 us
  waiting for transfers between devices  1260 us (59%)
  blocking collectives  354 us (17%)
  matrix products  218 us (10%)
  local copies, waits for them, and re-layouts  182 us (9%)
  other arithmetic  73.7 us (3%)
  starting transfers between devices  24.5 us (1%)
    all_gather x1, blocking collectives, local(): lax.all_gather(w_router, ('dp', 'expert'), axis=0, tiled=True)  275 us
    all_to_all x1, waiting for transfers between devices, local(): lax.all_to_all(row_grads, 'expert', split_axis=0, concat_axis=0, tiled=True)  166 us
    all_to_all x1, waiting for transfers between devices, local(): lax.all_to_all(result, 'expert', split_axis=0, concat_axis=0, tiled=True)  161 us
    all_to_all x1, waiting for transfers between devices, local(): lax.all_to_all(grad_outgoing, 'expert', split_axis=0, concat_axis=0, tile...  153 us
    reduce_scatter x1, waiting for transfers between devices, local(): lax.psum_scatter(out_w_grad, ('dp', 'expert'), scatter_dimension=0, tiled...  149 us
    reduce_scatter x1, waiting for transfers between devices, local(): lax.psum_scatter(query_w_grad, ('dp', 'expert'), scatter_dimension=0, til...  149 us
    reduce_scatter x1, waiting for transfers between devices, local(): lax.psum_scatter(value_w_grad, ('dp', 'expert'), scatter_dimension=0, til...  139 us
    reduce_scatter x1, waiting for transfers between devices, local(): lax.psum_scatter(key_w_grad, ('dp', 'expert'), scatter_dimension=0, tiled...  137 us
  transfers between devices with their start and end apart: 19, of which 12 were waited for; matrix products, arithmetic and copies ran while one was open for 19% of the time, Pallas kernels for 0%

commit v1 on v0

v1 whole, which is shorter than its diff:
```python
import math

import jax
import jax.numpy as jnp
from jax import lax
from jax.sharding import PartitionSpec as P

HEADS = 16
KV_HEADS = 8
HEAD_DIM = 64
EXPERTS = 32
CAP = 152


EPSILON = 1e-06


def rope_tables(length, head_width):
    half_width = head_width // 2
    ladder = jnp.arange(half_width, dtype=jnp.float32) * (2.0 / head_width)
    inverse = jnp.exp(-math.log(10000.0) * ladder)
    angles = jnp.arange(length, dtype=jnp.float32)[:, None] * inverse[None, :]
    return (jnp.cos(angles), jnp.sin(angles))


def rotate(values, cosine, sine_table):
    half_width = values.shape[-1] // 2
    first_half = values[..., :half_width]
    second = values[..., half_width:]
    cos_rows = cosine[:, None, :]
    sin_rows = sine_table[:, None, :]
    return jnp.concatenate(
        [first_half * cos_rows - second * sin_rows, second * cos_rows + first_half * sin_rows],
        axis=-1,
    )


def unrotate(grads, cosine, sine_table):
    half_width = grads.shape[-1] // 2
    first_half = grads[..., :half_width]
    second = grads[..., half_width:]
    cos_rows = cosine[:, None, :]
    sin_rows = sine_table[:, None, :]
    return jnp.concatenate(
        [first_half * cos_rows + second * sin_rows, second * cos_rows - first_half * sin_rows],
        axis=-1,
    )


def shift(array, axis, step):
    count = lax.axis_size(axis)
    return lax.ppermute(array, axis, [(i, (i + step) % count) for i in range(count)])


def take_rows(array, start, rows):
    return lax.dynamic_slice_in_dim(array, start, rows, axis=0)


def block_scores(query_block, keys, start, scale):
    scores = (
        jnp.einsum("qgrd,kgd->grqk", query_block, keys, preferred_element_type=jnp.float32) * scale
    )
    query_pos = start + jnp.arange(query_block.shape[0], dtype=jnp.int32)
    key_pos = jnp.arange(keys.shape[0], dtype=jnp.int32)
    return jnp.where(key_pos[None, :] <= query_pos[:, None], scores, -1e30)


def local(
    hidden_in,
    norm1_gain,
    w_query,
    w_key,
    w_value,
    w_out,
    norm2_gain,
    w_router,
    w_gate,
    w_up,
    w_down,
    expert_ids,
    out_grad,
):
    owners = lax.axis_size("expert")
    me = lax.axis_index("expert")
    local_experts = EXPERTS // owners
    experts = jnp.arange(EXPERTS, dtype=jnp.int32)
    mask = jnp.sum((expert_ids[:, :, None] == experts[None, None, :]).astype(jnp.float32), axis=1)
    shard = w_query.shape[0]
    tail = jnp.concatenate(
        [
            w_router,
            norm1_gain[:, None],
            norm2_gain[:, None],
            jnp.zeros((shard, 128 - EXPERTS - 2), jnp.bfloat16),
        ],
        axis=1,
    )
    dense = lax.all_gather(
        jnp.concatenate([w_query, w_key, w_value, w_out, tail], axis=1),
        ("dp", "expert"),
        axis=0,
        tiled=True,
    )
    q_end = HEADS * HEAD_DIM
    k_end = q_end + KV_HEADS * HEAD_DIM
    v_end = k_end + KV_HEADS * HEAD_DIM
    o_end = v_end + w_out.shape[1]
    qkv_w = dense[:, :v_end]
    out_w = dense[:, v_end:o_end]
    router_w = dense[:, o_end : o_end + EXPERTS]
    gain_one = dense[:, o_end + EXPERTS]
    gain_two = dense[:, o_end + EXPERTS + 1]
    down_shard = jnp.swapaxes(w_down, 1, 2)
    gate_w = lax.all_gather(w_gate, "dp", axis=1, tiled=True)
    up_w = lax.all_gather(w_up, "dp", axis=1, tiled=True)
    down_w = lax.all_gather(down_shard, "dp", axis=1, tiled=True)
    early = jnp.concatenate(
        [
            out_grad,
            mask.astype(jnp.bfloat16),
            jnp.zeros((mask.shape[0], 128 - EXPERTS), jnp.bfloat16),
        ],
        axis=1,
    )
    early_all = jnp.stack([early] + [shift(early, "expert", r) for r in range(1, owners)])
    inputs = hidden_in.astype(jnp.float32)
    length = inputs.shape[0]
    width = inputs.shape[1]
    group = HEADS // KV_HEADS
    scale = 1.0 / math.sqrt(HEAD_DIM)
    block_rows = min(512, length)
    cosine, sine_table = rope_tables(length, HEAD_DIM)
    factor_one = lax.rsqrt(jnp.mean(inputs * inputs, axis=-1, keepdims=True) + EPSILON)
    scaled_one = inputs * factor_one
    normed = (scaled_one * gain_one.astype(jnp.float32)).astype(jnp.bfloat16)
    qkv = jnp.dot(normed, qkv_w, preferred_element_type=jnp.float32)
    queries = qkv[:, :q_end].reshape(length, HEADS, HEAD_DIM)
    keys = qkv[:, q_end:k_end].reshape(length, KV_HEADS, HEAD_DIM)
    values_in = qkv[:, k_end:].astype(jnp.bfloat16).reshape(length, KV_HEADS, HEAD_DIM)
    queries = (
        rotate(queries, cosine, sine_table)
        .astype(jnp.bfloat16)
        .reshape(length, KV_HEADS, group, HEAD_DIM)
    )
    keys = rotate(keys, cosine, sine_table).astype(jnp.bfloat16)
    block_index = 0
    start = block_index * block_rows
    scores = block_scores(queries, keys, start, scale)
    top_score = jnp.max(scores, axis=-1, keepdims=True)
    log_total = top_score + jnp.log(jnp.sum(jnp.exp(scores - top_score), axis=-1, keepdims=True))
    weights = jnp.exp(scores - log_total).astype(jnp.bfloat16)
    pieces = jnp.einsum("grqk,kgd->qgrd", weights, values_in, preferred_element_type=jnp.float32)
    log_totals = [log_total]
    attended = pieces.reshape(length, HEADS * HEAD_DIM).astype(jnp.bfloat16)
    middle = inputs + jnp.dot(attended, out_w, preferred_element_type=jnp.float32)
    factor_two = lax.rsqrt(jnp.mean(middle * middle, axis=-1, keepdims=True) + EPSILON)
    scaled_two = middle * factor_two
    gain_float = gain_two.astype(jnp.float32)
    normed_two = (scaled_two * gain_float).astype(jnp.bfloat16)
    tokens = jnp.stack([normed_two] + [shift(normed_two, "expert", r) for r in range(1, owners)])
    grads_all = early_all[:, :, :width]
    mask_bf = early_all[:, :, width : width + EXPERTS]
    mask_all = mask_bf.astype(jnp.float32)
    order = jnp.arange(length, dtype=jnp.int32)
    before = (order[:, None] > order[None, :]).astype(jnp.bfloat16)
    mask_own = lax.dynamic_slice_in_dim(mask_bf, me * local_experts, local_experts, axis=2)
    ranks = jnp.einsum("stj,ut->sju", mask_own, before, preferred_element_type=jnp.float32)
    slots = jnp.where(
        jnp.swapaxes(mask_own, 1, 2) > 0, ranks.astype(jnp.int32), -1
    )
    places = slots[:, :, None, :] == jnp.arange(CAP, dtype=jnp.int32)[None, None, :, None]
    picks = places.astype(jnp.bfloat16)
    logits = jnp.einsum("std,de->ste", tokens, router_w, preferred_element_type=jnp.float32)
    masked = jnp.where(mask_all > 0, logits, -jnp.inf)
    raised = jnp.exp(masked - jnp.max(masked, axis=-1, keepdims=True))
    gates_all = raised / jnp.sum(raised, axis=-1, keepdims=True)
    gates = gates_all[0]
    gates_own = jnp.swapaxes(
        lax.dynamic_slice_in_dim(gates_all, me * local_experts, local_experts, axis=2), 1, 2
    )
    gate_slot = jnp.sum(jnp.where(places, gates_own[:, :, None, :], 0.0), axis=-1)
    grad_rows = jnp.einsum(
        "sjct,std->sjcd", picks, grads_all, preferred_element_type=jnp.float32
    ).astype(jnp.bfloat16)
    rows = jnp.einsum(
        "sjct,std->sjcd", picks, tokens, preferred_element_type=jnp.float32
    ).astype(jnp.bfloat16)
    gate_pre = jnp.einsum("sjcd,jdf->sjcf", rows, gate_w, preferred_element_type=jnp.float32)
    up_pre = jnp.einsum("sjcd,jdf->sjcf", rows, up_w, preferred_element_type=jnp.float32)
    sigmoid_gate = jax.nn.sigmoid(gate_pre)
    activated = gate_pre * sigmoid_gate
    hidden = (activated * up_pre).astype(jnp.bfloat16)
    arrived = (gate_slot[..., None] * grad_rows.astype(jnp.float32)).astype(jnp.bfloat16)
    down_grad = jnp.einsum("sjcd,sjcf->jdf", arrived, hidden, preferred_element_type=jnp.float32)
    down_total = lax.psum_scatter(
        down_grad.astype(jnp.bfloat16), "dp", scatter_dimension=1, tiled=True
    )
    result = jnp.einsum(
        "sjcf,jdf->sjcd", hidden, down_w, preferred_element_type=jnp.float32
    ).astype(jnp.bfloat16)
    result_float = result.astype(jnp.float32)
    weighted = (gate_slot[..., None] * result_float).astype(jnp.bfloat16)
    mixed_parts = jnp.einsum("sjct,sjcd->std", picks, weighted, preferred_element_type=jnp.float32)
    slot_grads = jnp.sum(grad_rows.astype(jnp.float32) * result_float, axis=-1)
    gate_grad_parts = jnp.sum(jnp.where(places, slot_grads[..., None], 0.0), axis=2)
    mixed = mixed_parts[0]
    gate_pieces = [gate_grad_parts[0]]
    for r in range(1, owners):
        mixed = mixed + shift(mixed_parts[r].astype(jnp.bfloat16), "expert", -r).astype(
            jnp.float32
        )
        gate_pieces.append(shift(gate_grad_parts[r], "expert", -r))
    layer_out = (middle + mixed).astype(jnp.bfloat16)
    gate_grads = jnp.roll(jnp.stack(gate_pieces), me, axis=0).reshape(EXPERTS, length).T
    upstream = out_grad.astype(jnp.float32)
    logit_grads = gates * (gate_grads - jnp.sum(gates * gate_grads, axis=-1, keepdims=True))
    logit_grads = logit_grads.astype(jnp.bfloat16)
    router_grad = jnp.einsum(
        "td,te->de", normed_two, logit_grads, preferred_element_type=jnp.float32
    )
    normed_grad = jnp.einsum("te,de->td", logit_grads, router_w, preferred_element_type=jnp.float32)
    hidden_grad = jnp.einsum("sjcd,jdf->sjcf", arrived, down_w, preferred_element_type=jnp.float32)
    gate_pre_grad = (
        hidden_grad * up_pre * sigmoid_gate * (1.0 + gate_pre * (1.0 - sigmoid_gate))
    ).astype(jnp.bfloat16)
    up_pre_grad = (hidden_grad * activated).astype(jnp.bfloat16)
    row_grads = jnp.einsum(
        "sjcf,jdf->sjcd", gate_pre_grad, gate_w, preferred_element_type=jnp.float32
    )
    row_grads = (
        row_grads
        + jnp.einsum("sjcf,jdf->sjcd", up_pre_grad, up_w, preferred_element_type=jnp.float32)
    ).astype(jnp.bfloat16)
    back_parts = jnp.einsum("sjct,sjcd->std", picks, row_grads, preferred_element_type=jnp.float32)
    gate_grad = jnp.einsum(
        "sjcd,sjcf->jdf", rows, gate_pre_grad, preferred_element_type=jnp.float32
    )
    up_grad = jnp.einsum("sjcd,sjcf->jdf", rows, up_pre_grad, preferred_element_type=jnp.float32)
    gate_total = lax.psum_scatter(
        gate_grad.astype(jnp.bfloat16), "dp", scatter_dimension=1, tiled=True
    ).astype(jnp.float32)
    up_total = lax.psum_scatter(
        up_grad.astype(jnp.bfloat16), "dp", scatter_dimension=1, tiled=True
    ).astype(jnp.float32)
    down_total = jnp.swapaxes(down_total.astype(jnp.float32), 1, 2)
    normed_grad = normed_grad + back_parts[0]
    for r in range(1, owners):
        normed_grad = normed_grad + shift(
            back_parts[r].astype(jnp.bfloat16), "expert", -r
        ).astype(jnp.float32)
    gain_two_grad = jnp.sum(normed_grad * scaled_two, axis=0)
    scaled_grad = normed_grad * gain_float
    middle_grad = upstream + factor_two * (
        scaled_grad - scaled_two * jnp.mean(scaled_grad * scaled_two, axis=-1, keepdims=True)
    )
    branch_grad = middle_grad.astype(jnp.bfloat16)
    out_w_grad = jnp.einsum("tk,td->kd", attended, branch_grad, preferred_element_type=jnp.float32)
    attended_grad = jnp.einsum(
        "td,kd->tk", branch_grad, out_w, preferred_element_type=jnp.float32
    ).astype(jnp.bfloat16)
    attended_grad = attended_grad.reshape(length, KV_HEADS, group, HEAD_DIM)
    key_grads = jnp.zeros((length, KV_HEADS, HEAD_DIM), jnp.float32)
    value_grads = jnp.zeros((length, KV_HEADS, HEAD_DIM), jnp.float32)
    block_index = 0
    start = block_index * block_rows
    key_len = start + block_rows
    scores = block_scores(queries, keys, start, scale)
    weights = jnp.exp(scores - log_totals[block_index])
    value_grads = value_grads.at[:key_len].add(
        jnp.einsum(
            "grqk,qgrd->kgd",
            weights.astype(jnp.bfloat16),
            attended_grad,
            preferred_element_type=jnp.float32,
        )
    )
    weight_grads = jnp.einsum(
        "qgrd,kgd->grqk", attended_grad, values_in, preferred_element_type=jnp.float32
    )
    centre = jnp.sum(weights * weight_grads, axis=-1, keepdims=True)
    score_grads = (weights * (weight_grads - centre)).astype(jnp.bfloat16)
    query_pieces = (
        jnp.einsum("grqk,kgd->qgrd", score_grads, keys, preferred_element_type=jnp.float32) * scale
    )
    key_grads = key_grads.at[:key_len].add(
        jnp.einsum("grqk,qgrd->kgd", score_grads, queries, preferred_element_type=jnp.float32)
        * scale
    )
    query_grads = query_pieces.reshape(length, HEADS, HEAD_DIM)
    query_grads = (
        unrotate(query_grads, cosine, sine_table)
        .reshape(length, HEADS * HEAD_DIM)
        .astype(jnp.bfloat16)
    )
    key_grads = (
        unrotate(key_grads, cosine, sine_table)
        .reshape(length, KV_HEADS * HEAD_DIM)
        .astype(jnp.bfloat16)
    )
    value_grads = value_grads.reshape(length, KV_HEADS * HEAD_DIM).astype(jnp.bfloat16)
    qkv_grads = jnp.concatenate([query_grads, key_grads, value_grads], axis=1)
    qkv_w_grad = jnp.einsum("td,tk->dk", normed, qkv_grads, preferred_element_type=jnp.float32)
    first_grad = jnp.einsum("tk,dk->td", qkv_grads, qkv_w, preferred_element_type=jnp.float32)
    gain_one_grad = jnp.sum(first_grad * scaled_one, axis=0)
    scaled_one_grad = first_grad * gain_one.astype(jnp.float32)
    input_grad = middle_grad + factor_one * (
        scaled_one_grad
        - scaled_one * jnp.mean(scaled_one_grad * scaled_one, axis=-1, keepdims=True)
    )
    tail_grad = jnp.concatenate(
        [
            router_grad,
            gain_one_grad[:, None],
            gain_two_grad[:, None],
            jnp.zeros((width, 128 - EXPERTS - 2), jnp.float32),
        ],
        axis=1,
    )
    dense_grad = jnp.concatenate(
        [
            qkv_w_grad.astype(jnp.bfloat16),
            out_w_grad.astype(jnp.bfloat16),
            tail_grad.astype(jnp.bfloat16),
        ],
        axis=1,
    )
    dense_part = lax.psum_scatter(dense_grad, "dp", scatter_dimension=0, tiled=True)
    total = take_rows(dense_part, me * shard, shard).astype(jnp.float32)
    for r in range(1, owners):
        piece = take_rows(dense_part, lax.rem(me + r, owners) * shard, shard)
        total = total + shift(piece, "expert", r).astype(jnp.float32)
    return (
        layer_out,
        input_grad.astype(jnp.bfloat16),
        total[:, o_end + EXPERTS],
        total[:, :q_end],
        total[:, q_end:k_end],
        total[:, k_end:v_end],
        total[:, v_end:o_end],
        total[:, o_end + EXPERTS + 1],
        total[:, o_end : o_end + EXPERTS],
        gate_total,
        up_total,
        down_total,
    )


def solution(mesh):
    return jax.shard_map(
        local,
        mesh=mesh,
        in_specs=(
            P(("dp", "expert"), None),
            P(("dp", "expert")),
            P(("dp", "expert"), None),
            P(("dp", "expert"), None),
            P(("dp", "expert"), None),
            P(("dp", "expert"), None),
            P(("dp", "expert")),
            P(("dp", "expert"), None),
            P("expert", "dp", None),
            P("expert", "dp", None),
            P("expert", None, "dp"),
            P(("dp", "expert"), None),
            P(("dp", "expert"), None),
        ),
        out_specs=(
            P(("dp", "expert"), None),
            P(("dp", "expert"), None),
            P(("dp", "expert")),
            P(("dp", "expert"), None),
            P(("dp", "expert"), None),
            P(("dp", "expert"), None),
            P(("dp", "expert"), None),
            P(("dp", "expert")),
            P(("dp", "expert"), None),
            P("expert", "dp", None),
            P("expert", "dp", None),
            P("expert", None, "dp"),
        ),
        check_vma=False,
    )
```

time: 2130 us -> 948 us (0.45)
  waiting for transfers between devices: 1260 us -> 504 us
  blocking collectives: 354 us -> 0 us
  local copies, waits for them, and re-layouts: 182 us -> 43.9 us
  starting transfers between devices: 24.5 us -> 80.4 us
  matrix products: 218 us -> 246 us
  other arithmetic: 73.7 us -> 46.4 us
    reduce_scatter x5 -> x2, waiting for transfers between devices: 617 us -> 70.2 us  [the longest x1 52.5 us: local(): lax.psum_scatter(down_grad.astype(jnp.bfloat16), 'dp', scatter_dimension=...]
    all_to_all x4 -> x0, waiting for transfers between devices: 481 us -> none  [the longest x1 166 us: local(): lax.all_to_all(row_grads, 'expert', split_axis=0, concat_axis=0, tiled=True)]
    all_gather x1 -> x0, blocking collectives: 275 us -> none  [local(): lax.all_gather(w_router, ('dp', 'expert'), axis=0, tiled=True)]
    ppermute x0 -> x18, waiting for transfers between devices: none -> 151 us  [shift(): lax.ppermute(array, axis, [(i, (i + step) % count) for i in range(count)])]
    gather x4 -> x0, local copies, waits for them, and re-layouts: 94.2 us -> none  [the longest x1 26.2 us: local(): grad_outgoing = grad_rows[table].reshape(owners, local_experts, CAP, width)]
    ppermute x0 -> x18, starting transfers between devices: none -> 80 us  [shift(): lax.ppermute(array, axis, [(i, (i + step) % count) for i in range(count)])]
    unnamed x2 -> x0, blocking collectives: 79.1 us -> none
    reduce_scatter x1, waiting for transfers between devices: 0.01 us -> 72.3 us  [local(): lax.psum_scatter(up_grad.astype(jnp.bfloat16), 'dp', scatter_dimension=1,...]
  transfers between devices with their start and end apart: 19 -> 26, of which waited for: 12 -> 12; matrix products, arithmetic and copies ran while one was open for 19% -> 23% of each run, Pallas kernels for 0% -> 0%
where the time goes in v1:
time: 948 us; the launch traced here: 937 us
  waiting for transfers between devices  504 us (53%)
  matrix products  246 us (26%)
  starting transfers between devices  80.4 us (8%)
  other arithmetic  46.4 us (5%)
  local copies, waits for them, and re-layouts  43.9 us (5%)
  between operations  15.5 us (2%)
    ppermute x18, waiting for transfers between devices, shift(): lax.ppermute(array, axis, [(i, (i + step) % count) for i in range(count)])  151 us
    all_gather x1, waiting for transfers between devices, local(): lax.all_gather(jnp.concatenate([w_query, w_key, w_value, w_out, tail], ax...  128 us
    ppermute x18, starting transfers between devices, shift(): lax.ppermute(array, axis, [(i, (i + step) % count) for i in range(count)])  80 us
    reduce_scatter x1, waiting for transfers between devices, local(): lax.psum_scatter(up_grad.astype(jnp.bfloat16), 'dp', scatter_dimension=1,...  72.3 us
    reduce_scatter x1, waiting for transfers between devices, local(): lax.psum_scatter(gate_grad.astype(jnp.bfloat16), 'dp', scatter_dimension=...  71.4 us
    reduce_scatter x1, waiting for transfers between devices, local(): lax.psum_scatter(down_grad.astype(jnp.bfloat16), 'dp', scatter_dimension=...  52.5 us
    dot_general x1, matrix products, local(): jnp.einsum('sjct,sjcd->std', picks, row_grads, preferred_element_type=jnp...  21.5 us
  transfers between devices with their start and end apart: 26, of which 12 were waited for; matrix products, arithmetic and copies ran while one was open for 23% of the time, Pallas kernels for 0%

profile of v1, /device:TPU:0, one launch (start us, length us, event | category | flops | bytes accessed | tf_op | source)
XLA Modules:
  0.0 937.0 jit_solution(5817330081247142287)
XLA Ops:
  24.6 128.4 %all-gather.5.cloned.1.call-done = bf16[1024,3200]{1,0:T(8,128)(2,1)} async-done(((bf16[32,3200]{1,0:T(8,128)(2,1)}), bf16[1024,3200]{1,0:T(8,128)(2,1)}) %all-gather.5.cloned.1.call-update) | async-done | bytes 6553616 | tf_op jit(solution)/shard_map/all_gather | solution.py:98
  168.4 7.3 fusion.160
  175.8 8.2 exponential_reduce_fusion
  184.0 9.1 fusion.115
  206.0 21.5 %collective-permute-done.3 = bf16[512,1024]{1,0:T(8,128)(2,1)} collective-permute-done((bf16[512,1024]{1,0:T(8,128)(2,1)}, bf16[512,1024]{1,0:T(8,128)(2,1)}, u32[]{:S(2)}, u32[]{:S(2)}) %collective-permute-start.3) | collective-permute-done | bytes 1048608 | tf_op jit(solution)/shard_map/ppermute | solution.py:52
  227.4 44.5 %collective-permute-done.4 = bf16[512,1024]{1,0:T(8,128)(2,1)} collective-permute-done((bf16[512,1024]{1,0:T(8,128)(2,1)}, bf16[512,1024]{1,0:T(8,128)(2,1)}, u32[]{:S(2)}, u32[]{:S(2)}) %collective-permute-start.4) | collective-permute-done | bytes 1048608 | tf_op jit(solution)/shard_map/ppermute | solution.py:52
  275.4 9.6 %fusion.54 = bf16[4,8,152,1024]{3,2,1,0:T(8,128)(2,1)} fusion(s32[4,8,512]{2,1,0:T(8,128)S(1)} %fusion.128, bf16[1,512,1024]{2,1,0:T(8,128)(2,1)} %bitcast.23, bf16[1,512,1024]{2,1,0:T(8,128)(2,1)} %bitcast.22, bf16[1,512,1024]{2,1,0:T(8,128)(2,1)} %bitcast.21, bf16[1,512,1024]{2,1,0:T(8,128)(2,1)S(1)} %copy-done.26), kind=kOutput, calls=%fused_computation.62 | convolution fusion | flops 5114036224 | bytes 14221312 | tf_op jit(solution)/shard_map/sjct,std->sjcd/dot_general | solution.py:185
  285.0 13.3 %fusion.27 = f32[8,4,152,512]{3,2,1,0:T(8,128)} fusion(bf16[4,8,152,1024]{3,2,1,0:T(8,128)(2,1)} %fusion.54, bf16[8,1024,512]{2,1,0:T(8,128)(2,1)} %all-gather.7.cloned.1.call-done), kind=kOutput, calls=%fused_computation.47 | convolution fusion | flops 5100273664 | bytes 28311552 | tf_op jit(solution)/shard_map/sjcd,jdf->sjcf/dot_general | solution.py:188
  298.4 15.7 %fusion.15 = (bf16[4,8,152,512]{3,2,0,1:T(8,128)(2,1)}, f32[8,4,152,512]{3,2,1,0:T(8,128)}) fusion(f32[8,4,152,512]{3,2,1,0:T(8,128)} %fusion.27, bf16[8,1024,512]{2,1,0:T(8,128)(2,1)} %all-gather.9.cloned.1.call-done, bf16[4,8,152,1024]{3,2,1,0:T(8,128)(2,1)} %fusion.54), kind=kOutput, calls=%fused_computation.29 | convolution fusion | flops 5115215872 | bytes 43253760 | tf_op jit(solution)/shard_map/sjcd,jdf->sjcf/dot_general | solution.py:189
  314.0 9.1 all-gather.11.cloned.1.call-done
  323.2 11.9 %fusion.48 = bf16[8,4,152,1024]{3,2,1,0:T(8,128)(2,1)} fusion(bf16[4,8,152,512]{3,2,0,1:T(8,128)(2,1)} %get-tuple-element.171, bf16[8,1024,512]{2,1,0:T(8,128)(2,1)} %all-gather.11.cloned.1.call-done), kind=kOutput, calls=%fused_computation.60 | convolution fusion | flops 5105254400 | bytes 23330816 | tf_op jit(solution)/shard_map/sjcf,jdf->sjcd/dot_general | solution.py:198
  335.1 11.8 %fusion.1 = (f32[4,8,152]{2,0,1:T(4,128)S(1)}, bf16[4,8,152,1024]{3,2,0,1:T(8,128)(2,1)}) fusion(bf16[8,4,152,1024]{3,2,1,0:T(8,128)(2,1)} %fusion.48, bf16[1,512,1152]{1,2,0:T(8,128)(2,1)} %bitcast.17, bf16[1,512,1152]{1,2,0:T(8,128)(2,1)} %bitcast.16, bf16[1,512,1152]{1,2,0:T(8,128)(2,1)} %bitcast.15, bf16[1,512,1152]{1,2,0:T(8,128)(2,1)S(1)} %copy-done.8, ...), kind=kOutput, calls=%fused_computation.3 | convolution fusion | flops 5144439808 | bytes 24726528 | tf_op jit(solution)/shard_map/sjct,std->sjcd/dot_general | solution.py:182
  350.9 10.7 %fusion.167 = (bf16[4,512,1024]{2,1,0:T(8,128)(2,1)S(1)}, f32[4,512,1024]{2,1,0:T(8,128)}) fusion(s32[4,8,512]{2,1,0:T(8,128)S(1)} %fusion.128, bf16[8,4,152,1024]{3,2,1,0:T(8,128)(2,1)} %fusion.48, f32[4,8,152]{2,0,1:T(4,128)S(1)} %copy.186), kind=kOutput, calls=%fused_computation.223 | convolution fusion | flops 5119803392 | bytes 22629376 | tf_op jit(solution)/shard_map/sjct,sjcd->std/dot_general | solution.py:203
  363.3 8.2 collective-permute-start.6
  371.5 6.9 collective-permute-start.7
  380.4 18.6 %fusion.13 = (bf16[4,8,152,512]{3,2,0,1:T(8,128)(2,1)}, bf16[4,8,152,512]{3,2,0,1:T(8,128)(2,1)}) fusion(f32[8,4,152,512]{3,2,1,0:T(8,128)} %get-tuple-element.172, f32[8,4,152,512]{3,2,1,0:T(8,128)} %fusion.27, bf16[8,1024,512]{2,1,0:T(8,128)(2,1)} %all-gather.11.cloned.1.call-done, bf16[4,8,152,1024]{3,2,0,1:T(8,128)(2,1)} %get-tuple-element.174, ...), kind=kOutput, calls=%fused_computation.26 | convolution fusion | flops 5147590656 | bytes 48253952 | tf_op jit(solution)/shard_map/sjcd,jdf->sjcf/dot_general | solution.py:222
  399.0 13.6 %fusion.38 = f32[8,4,152,1024]{3,2,0,1:T(8,128)} fusion(bf16[8,1024,512]{2,1,0:T(8,128)(2,1)} %all-gather.9.cloned.1.call-done, bf16[4,8,152,512]{3,2,0,1:T(8,128)(2,1)} %get-tuple-element.135), kind=kOutput, calls=%fused_computation.56 | convolution fusion | flops 5100273664 | bytes 33292288 | tf_op jit(solution)/shard_map/sjcf,jdf->sjcd/dot_general | solution.py:232
  412.7 21.5 %fusion.162 = (bf16[4,512,1024]{2,1,0:T(8,128)(2,1)}, f32[4,512,1024]{2,1,0:T(8,128)}) fusion(f32[8,4,152,1024]{3,2,0,1:T(8,128)} %fusion.38, bf16[8,1024,512]{2,1,0:T(8,128)(2,1)} %all-gather.7.cloned.1.call-done, bf16[4,8,152,512]{3,2,0,1:T(8,128)(2,1)} %get-tuple-element.134, s32[4,8,512]{2,1,0:T(8,128)S(1)} %fusion.128), kind=kOutput, calls=%fused_computation.222 | convolution fusion | flops 10215096320 | bytes 45940736 | tf_op jit(solution)/shard_map/sjct,sjcd->std/dot_general | solution.py:234
  440.5 7.5 collective-permute-done.10
  449.9 40.2 %collective-permute-start.14 = (bf16[512,1024]{1,0:T(8,128)(2,1)}, bf16[512,1024]{1,0:T(8,128)(2,1)}, u32[]{:S(2)}, u32[]{:S(2)}) collective-permute-start(bf16[512,1024]{1,0:T(8,128)(2,1)} %get-tuple-element.137), channel_id=1, source_target_pairs={{0,1},{1,2},{2,3},{3,0},{4,5},{5,6},{6,7},{7,4},{8,9},{9,10},{10,1... | collective-permute-start | bytes 3145736 | tf_op jit(solution)/shard_map/ppermute | solution.py:52
  492.8 68.9 %collective-permute-done.13 = bf16[512,1024]{1,0:T(8,128)(2,1)} collective-permute-done((bf16[512,1024]{1,0:T(8,128)(2,1)}, bf16[512,1024]{1,0:T(8,128)(2,1)}, u32[]{:S(2)}, u32[]{:S(2)}) %collective-permute-start.13) | collective-permute-done | bytes 1048608 | tf_op jit(solution)/shard_map/ppermute | solution.py:52
  576.9 15.4 %fusion.4 = (f32[8,2,512]{2,1,0:T(2,128)S(1)}, f32[8,512,512,2]{2,1,3,0:T(8,128)}) fusion(f32[8,2,512,512]{2,3,1,0:T(8,128)} %get-tuple-element.168, f32[8,2,512]{2,1,0:T(2,128)S(1)} %bitcast.297, bf16[512,8,64,1]{0,2,3,1:T(8,128)(2,1)S(1)} %bitcast.285, bf16[512,8,2,64]{0,3,2,1:T(8,128)(2,1)S(1)} %bitcast.280), kind=kOutput, calls=%fused_computation.13 | convolution fusion | flops 549445632 | bytes 35192832 | tf_op jit(solution)/shard_map/qgrd,kgd->grqk/dot_general | solution.py:277
  593.0 8.3 fusion.6
  632.5 10.4 %concatenate.55 = bf16[1024,3200]{1,0:T(8,128)(2,1)} concatenate(bf16[1024,2048]{1,0:T(8,128)(2,1)} %convolution_convert_fusion, bf16[1024,1024]{1,0:T(8,128)(2,1)S(1)} %copy-done.19, bf16[1024,32]{1,0:T(8,128)(2,1)S(1)} %copy.201, bf16[1024,1]{1,0:T(8,128)(2,1)S(1)} %broadcast_in_dim.115, bf16[1024,1]{1,0:T(8,128)(2,1)S(1)} %broadcast_in_dim.116, ...), dimensions={1} | concatenate | bytes 13107200 | tf_op jit(solution)/shard_map/concatenate | solution.py:319
  642.9 15.1 %bitcast_convert_fusion = bf16[8,1024,512]{2,1,0:T(8,128)(2,1)} fusion(bf16[4,8,152,512]{3,2,0,1:T(8,128)(2,1)} %get-tuple-element.171, bf16[4,8,152,1024]{3,2,0,1:T(8,128)(2,1)} %get-tuple-element.174, f32[4,8,152]{2,0,1:T(4,128)S(1)} %copy.186), kind=kOutput, calls=%fused_computation.8 | convolution fusion | flops 5119410176 | bytes 23350272 | tf_op jit(solution)/shard_map/sjcd,sjcf->jdf/dot_general | solution.py:194
  658.1 13.1 %bitcast_convert_fusion.2 = bf16[8,1024,512]{2,1,0:T(8,128)(2,1)} fusion(bf16[4,8,152,1024]{3,2,1,0:T(8,128)(2,1)} %fusion.54, bf16[4,8,152,512]{3,2,0,1:T(8,128)(2,1)} %get-tuple-element.134), kind=kOutput, calls=%fused_computation.10 | convolution fusion | flops 5104467968 | bytes 23330816 | tf_op jit(solution)/shard_map/sjcd,sjcf->jdf/dot_general | solution.py:235
  671.3 12.9 %bitcast_convert_fusion.1 = bf16[8,1024,512]{2,1,0:T(8,128)(2,1)} fusion(bf16[4,8,152,1024]{3,2,1,0:T(8,128)(2,1)} %fusion.54, bf16[4,8,152,512]{3,2,0,1:T(8,128)(2,1)} %get-tuple-element.135), kind=kOutput, calls=%fused_computation.9 | convolution fusion | flops 5104467968 | bytes 23330816 | tf_op jit(solution)/shard_map/sjcd,sjcf->jdf/dot_general | solution.py:238
  684.2 17.7 %reduce-scatter.5.cloned.1.call-done = bf16[128,3200]{1,0:T(8,128)(2,1)} async-done(((bf16[1024,3200]{1,0:T(8,128)(2,1)}), bf16[128,3200]{1,0:T(8,128)(2,1)}) %reduce-scatter.5.cloned.1.call-update) | async-done | bytes 819216 | tf_op jit(solution)/shard_map/reduce_scatter | solution.py:327
  713.0 7.6 collective-permute-done.16
  724.4 52.5 %reduce-scatter.11.cloned.1.call-done = bf16[8,128,512]{2,1,0:T(8,128)(2,1)} async-done(((bf16[8,1024,512]{2,1,0:T(8,128)(2,1)}), bf16[8,128,512]{2,1,0:T(8,128)(2,1)}) %reduce-scatter.11.cloned.1.call-update) | async-done | bytes 1048592 | tf_op jit(solution)/shard_map/reduce_scatter | solution.py:195
  780.2 71.4 %reduce-scatter.7.cloned.1.call-done = bf16[8,128,512]{2,1,0:T(8,128)(2,1)} async-done(((bf16[8,1024,512]{2,1,0:T(8,128)(2,1)}), bf16[8,128,512]{2,1,0:T(8,128)(2,1)}) %reduce-scatter.7.cloned.1.call-update) | async-done | bytes 1048592 | tf_op jit(solution)/shard_map/reduce_scatter | solution.py:239
  854.5 72.3 %reduce-scatter.9.cloned.1.call-done = bf16[8,128,512]{2,1,0:T(8,128)(2,1)} async-done(((bf16[8,1024,512]{2,1,0:T(8,128)(2,1)}), bf16[8,128,512]{2,1,0:T(8,128)(2,1)}) %reduce-scatter.9.cloned.1.call-update) | async-done | bytes 1048592 | tf_op jit(solution)/shard_map/reduce_scatter | solution.py:242
  (232 shorter events, 138.1 us)
Async XLA Ops:
  7.2 145.8 %all-gather.5.cloned.1.call-start = ((), (), s32[]{:S(2)}) async-start(), calls=%async_computation.4 | async-start | bytes 6758400 | tf_op jit(solution)/shard_map/all_gather | solution.py:98
  10.5 274.5 %all-gather.7.cloned.1.call-start = ((), (), s32[]{:S(2)}) async-start(), calls=%async_computation.5 | async-start | bytes 9437184 | tf_op jit(solution)/shard_map/all_gather | solution.py:114
  11.3 287.1 %all-gather.9.cloned.1.call-start = ((), (), s32[]{:S(2)}) async-start(), calls=%async_computation.6 | async-start | bytes 9437184 | tf_op jit(solution)/shard_map/all_gather | solution.py:115
  12.0 311.1 %all-gather.11.cloned.1.call-start = ((), (), s32[]{:S(2)}) async-start(), calls=%async_computation.7 | async-start | bytes 9437184 | tf_op jit(solution)/shard_map/all_gather | solution.py:116
  14.4 687.5 %reduce-scatter.5.cloned.1.call-start = ((), (), s32[]{:S(2)}) async-start(), calls=%async_computation.8 | async-start | bytes 7372800 | tf_op jit(solution)/shard_map/reduce_scatter | solution.py:327
  16.9 186.8 %collective-permute-start = (bf16[512,1152]{0,1:T(8,128)(2,1)}, bf16[512,1152]{0,1:T(8,128)(2,1)}, u32[]{:S(2)}, u32[]{:S(2)}) collective-permute-start(bf16[512,1152]{0,1:T(8,128)(2,1)} %get-tuple-element.153), channel_id=1, source_target_pairs={{0,1},{1,2},{2,3},{3,0},{4,5},{5,6},{6,7},{7,4},{8,9},{9,10},{10,1... | collective-permute-start | bytes 3538952 | tf_op jit(solution)/shard_map/ppermute | solution.py:52
  19.9 183.7 %collective-permute-start.1 = (bf16[512,1152]{0,1:T(8,128)(2,1)}, bf16[512,1152]{0,1:T(8,128)(2,1)}, u32[]{:S(2)}, u32[]{:S(2)}) collective-permute-start(bf16[512,1152]{0,1:T(8,128)(2,1)} %get-tuple-element.153), channel_id=1, source_target_pairs={{0,2},{1,3},{2,0},{3,1},{4,6},{5,7},{6,4},{7,5},{8,10},{9,11},{10,... | collective-permute-start | bytes 3538952 | tf_op jit(solution)/shard_map/ppermute | solution.py:52
  22.5 181.1 %collective-permute-start.2 = (bf16[512,1152]{0,1:T(8,128)(2,1)}, bf16[512,1152]{0,1:T(8,128)(2,1)}, u32[]{:S(2)}, u32[]{:S(2)}) collective-permute-start(bf16[512,1152]{0,1:T(8,128)(2,1)} %get-tuple-element.153), channel_id=1, source_target_pairs={{0,3},{1,0},{2,1},{3,2},{4,7},{5,4},{6,5},{7,6},{8,11},{9,8},{10,9... | collective-permute-start | bytes 3538952 | tf_op jit(solution)/shard_map/ppermute | solution.py:52
  24.2 134.8 %copy-start.43 = (f32[512]{0:T(512)}, f32[512]{0:T(512)S(1)}, u32[]{:S(2)}) copy-start(f32[512]{0:T(512)S(1)} %add_rsqrt_fusion.1) | copy-start | bytes 6148
  24.5 143.5 %copy-start.20 = (f32[512,32]{0,1:T(8,128)}, f32[512,32]{0,1:T(8,128)S(1)}, u32[]{:S(2)}) copy-start(f32[512,32]{0,1:T(8,128)S(1)} %get-tuple-element.165) | copy-start | bytes 196612
  24.6 143.5 %copy-start.22 = (f32[512,32]{0,1:T(8,128)}, f32[512,32]{0,1:T(8,128)S(1)}, u32[]{:S(2)}) copy-start(f32[512,32]{0,1:T(8,128)S(1)} %get-tuple-element.166) | copy-start | bytes 196612
  198.0 29.5 %collective-permute-start.3 = (bf16[512,1024]{1,0:T(8,128)(2,1)}, bf16[512,1024]{1,0:T(8,128)(2,1)}, u32[]{:S(2)}, u32[]{:S(2)}) collective-permute-start(bf16[512,1024]{1,0:T(8,128)(2,1)} %multiply_convert_fusion), channel_id=1, source_target_pairs={{0,1},{1,2},{2,3},{3,0},{4,5},{5,6},{6,7},{7,4},{8,9},{9,10},{10,1... | collective-permute-start | bytes 3145736 | tf_op jit(solution)/shard_map/ppermute | solution.py:52
  198.2 73.8 %collective-permute-start.4 = (bf16[512,1024]{1,0:T(8,128)(2,1)}, bf16[512,1024]{1,0:T(8,128)(2,1)}, u32[]{:S(2)}, u32[]{:S(2)}) collective-permute-start(bf16[512,1024]{1,0:T(8,128)(2,1)} %multiply_convert_fusion), channel_id=1, source_target_pairs={{0,2},{1,3},{2,0},{3,1},{4,6},{5,7},{6,4},{7,5},{8,10},{9,11},{10,... | collective-permute-start | bytes 3145736 | tf_op jit(solution)/shard_map/ppermute | solution.py:52
  203.6 68.3 %collective-permute-start.5 = (bf16[512,1024]{1,0:T(8,128)(2,1)}, bf16[512,1024]{1,0:T(8,128)(2,1)}, u32[]{:S(2)}, u32[]{:S(2)}) collective-permute-start(bf16[512,1024]{1,0:T(8,128)(2,1)} %multiply_convert_fusion), channel_id=1, source_target_pairs={{0,3},{1,0},{2,1},{3,2},{4,7},{5,4},{6,5},{7,6},{8,11},{9,8},{10,9... | collective-permute-start | bytes 3145736 | tf_op jit(solution)/shard_map/ppermute | solution.py:52
  363.3 202.2 %collective-permute-start.6 = (bf16[512,1024]{1,0:T(8,128)(2,1)}, bf16[512,1024]{1,0:T(8,128)(2,1)}, u32[]{:S(2)}, u32[]{:S(2)}) collective-permute-start(bf16[512,1024]{1,0:T(8,128)(2,1)} %get-tuple-element.139), channel_id=1, source_target_pairs={{0,3},{1,0},{2,1},{3,2},{4,7},{5,4},{6,5},{7,6},{8,11},{9,8},{10,9... | collective-permute-start | bytes 3145736 | tf_op jit(solution)/shard_map/ppermute | solution.py:52
  371.5 194.1 %collective-permute-start.7 = (bf16[512,1024]{1,0:T(8,128)(2,1)}, bf16[512,1024]{1,0:T(8,128)(2,1)}, u32[]{:S(2)}, u32[]{:S(2)}) collective-permute-start(bf16[512,1024]{1,0:T(8,128)(2,1)} %get-tuple-element.141), channel_id=1, source_target_pairs={{0,2},{1,3},{2,0},{3,1},{4,6},{5,7},{6,4},{7,5},{8,10},{9,11},{10,... | collective-permute-start | bytes 3145736 | tf_op jit(solution)/shard_map/ppermute | solution.py:52
  378.4 59.5 %collective-permute-start.9 = (f32[8,512]{1,0:T(8,128)S(1)}, f32[8,512]{1,0:T(8,128)S(1)}, u32[]{:S(2)}, u32[]{:S(2)}) collective-permute-start(f32[8,512]{1,0:T(8,128)S(1)} %get-tuple-element.164), channel_id=1, source_target_pairs={{0,3},{1,0},{2,1},{3,2},{4,7},{5,4},{6,5},{7,6},{8,11},{9,8},{10,9... | collective-permute-start | bytes 49160 | tf_op jit(solution)/shard_map/ppermute | solution.py:52
  379.3 68.8 %collective-permute-start.10 = (f32[8,512]{1,0:T(8,128)S(1)}, f32[8,512]{1,0:T(8,128)S(1)}, u32[]{:S(2)}, u32[]{:S(2)}) collective-permute-start(f32[8,512]{1,0:T(8,128)S(1)} %get-tuple-element.163), channel_id=1, source_target_pairs={{0,2},{1,3},{2,0},{3,1},{4,6},{5,7},{6,4},{7,5},{8,10},{9,11},{10,... | collective-permute-start | bytes 49160 | tf_op jit(solution)/shard_map/ppermute | solution.py:52
  379.3 70.6 %collective-permute-start.11 = (f32[8,512]{1,0:T(8,128)S(1)}, f32[8,512]{1,0:T(8,128)S(1)}, u32[]{:S(2)}, u32[]{:S(2)}) collective-permute-start(f32[8,512]{1,0:T(8,128)S(1)} %get-tuple-element.161), channel_id=1, source_target_pairs={{0,1},{1,2},{2,3},{3,0},{4,5},{5,6},{6,7},{7,4},{8,9},{9,10},{10,1... | collective-permute-start | bytes 49160 | tf_op jit(solution)/shard_map/ppermute | solution.py:52
  434.2 127.5 %copy-start.2 = (f32[512,1024]{1,0:T(8,128)S(1)}, f32[512,1024]{1,0:T(8,128)}, u32[]{:S(2)}) copy-start(f32[512,1024]{1,0:T(8,128)} %copy-done.1) | copy-start | bytes 6291460
  434.2 127.5 %copy-start.37 = (f32[1024]{0:T(1024)S(1)}, f32[1024]{0:T(1024)}, u32[]{:S(2)}) copy-start(f32[1024]{0:T(1024)} %copy-done.36) | copy-start | bytes 12292
  434.2 127.5 %copy-start.39 = (f32[512]{0:T(512)S(1)}, f32[512]{0:T(512)}, u32[]{:S(2)}) copy-start(f32[512]{0:T(512)} %copy-done.38) | copy-start | bytes 6148
  437.8 52.3 %collective-permute-start.12 = (bf16[512,1024]{1,0:T(8,128)(2,1)S(1)}, bf16[512,1024]{1,0:T(8,128)(2,1)S(1)}, u32[]{:S(2)}, u32[]{:S(2)}) collective-permute-start(bf16[512,1024]{1,0:T(8,128)(2,1)S(1)} %get-tuple-element.136), channel_id=1, source_target_pairs={{0,3},{1,0},{2,1},{3,2},{4,7},{5,4},{6,5},{7,6},{8,11},{9,8},{10,9... | collective-permute-start | bytes 3145736 | tf_op jit(solution)/shard_map/ppermute | solution.py:52
  448.0 113.6 %collective-permute-start.13 = (bf16[512,1024]{1,0:T(8,128)(2,1)}, bf16[512,1024]{1,0:T(8,128)(2,1)}, u32[]{:S(2)}, u32[]{:S(2)}) collective-permute-start(bf16[512,1024]{1,0:T(8,128)(2,1)} %get-tuple-element.138), channel_id=1, source_target_pairs={{0,2},{1,3},{2,0},{3,1},{4,6},{5,7},{6,4},{7,5},{8,10},{9,11},{10,... | collective-permute-start | bytes 3145736 | tf_op jit(solution)/shard_map/ppermute | solution.py:52
  449.9 111.8 %collective-permute-start.14 = (bf16[512,1024]{1,0:T(8,128)(2,1)}, bf16[512,1024]{1,0:T(8,128)(2,1)}, u32[]{:S(2)}, u32[]{:S(2)}) collective-permute-start(bf16[512,1024]{1,0:T(8,128)(2,1)} %get-tuple-element.137), channel_id=1, source_target_pairs={{0,1},{1,2},{2,3},{3,0},{4,5},{5,6},{6,7},{7,4},{8,9},{9,10},{10,1... | collective-permute-start | bytes 3145736 | tf_op jit(solution)/shard_map/ppermute | solution.py:52
  490.2 75.4 %collective-permute-start.8 = (bf16[512,1024]{1,0:T(8,128)(2,1)}, bf16[512,1024]{1,0:T(8,128)(2,1)}, u32[]{:S(2)}, u32[]{:S(2)}) collective-permute-start(bf16[512,1024]{1,0:T(8,128)(2,1)} %get-tuple-element.140), channel_id=1, source_target_pairs={{0,1},{1,2},{2,3},{3,0},{4,5},{5,6},{6,7},{7,4},{8,9},{9,10},{10,1... | collective-permute-start | bytes 3145736 | tf_op jit(solution)/shard_map/ppermute | solution.py:52
  642.9 134.1 %reduce-scatter.11.cloned.1.call-start = ((), (), s32[]{:S(2)}) async-start(), calls=%async_computation.11 | async-start | bytes 9437184 | tf_op jit(solution)/shard_map/reduce_scatter | solution.py:195
  658.0 193.6 %reduce-scatter.7.cloned.1.call-start = ((), (), s32[]{:S(2)}) async-start(), calls=%async_computation.9 | async-start | bytes 9437184 | tf_op jit(solution)/shard_map/reduce_scatter | solution.py:239
  671.2 255.6 %reduce-scatter.9.cloned.1.call-start = ((), (), s32[]{:S(2)}) async-start(), calls=%async_computation.10 | async-start | bytes 9437184 | tf_op jit(solution)/shard_map/reduce_scatter | solution.py:242
  703.1 10.0 %collective-permute-start.15 = (bf16[32,3200]{1,0:T(8,128)(2,1)S(1)}, bf16[32,3200]{1,0:T(8,128)(2,1)S(1)}, u32[]{:S(2)}, u32[]{:S(2)}) collective-permute-start(bf16[32,3200]{1,0:T(8,128)(2,1)S(1)} %get-tuple-element.154), channel_id=1, source_target_pairs={{0,1},{1,2},{2,3},{3,0},{4,5},{5,6},{6,7},{7,4},{8,9},{9,10},{10,1... | collective-permute-start | bytes 614408 | tf_op jit(solution)/shard_map/ppermute | solution.py:52
  704.6 16.0 %collective-permute-start.16 = (bf16[32,3200]{1,0:T(8,128)(2,1)S(1)}, bf16[32,3200]{1,0:T(8,128)(2,1)S(1)}, u32[]{:S(2)}, u32[]{:S(2)}) collective-permute-start(bf16[32,3200]{1,0:T(8,128)(2,1)S(1)} %get-tuple-element.156), channel_id=1, source_target_pairs={{0,2},{1,3},{2,0},{3,1},{4,6},{5,7},{6,4},{7,5},{8,10},{9,11},{10,... | collective-permute-start | bytes 614408 | tf_op jit(solution)/shard_map/ppermute | solution.py:52
  707.1 13.6 %collective-permute-start.17 = (bf16[32,3200]{1,0:T(8,128)(2,1)S(1)}, bf16[32,3200]{1,0:T(8,128)(2,1)S(1)}, u32[]{:S(2)}, u32[]{:S(2)}) collective-permute-start(bf16[32,3200]{1,0:T(8,128)(2,1)S(1)} %get-tuple-element.155), channel_id=1, source_target_pairs={{0,3},{1,0},{2,1},{3,2},{4,7},{5,4},{6,5},{7,6},{8,11},{9,8},{10,9... | collective-permute-start | bytes 614408 | tf_op jit(solution)/shard_map/ppermute | solution.py:52
  (45 other events, 518.4 us)
Sparse Core Ops, SparseCore 0:
  11.4 141.5 all-gather.4
  154.9 55.6 all-gather.6
  212.5 54.3 all-gather.8
  268.7 54.3 all-gather.10
  643.0 58.8 reduce-scatter.4
  705.6 71.2 reduce-scatter.10
  780.4 71.2 reduce-scatter.6
  855.5 71.2 reduce-scatter.8

commit v2 on v1

--- a/solution.py
+++ b/solution.py
@@ -3,6 +3,7 @@
 import jax
 import jax.numpy as jnp
 from jax import lax
+from jax.experimental.layout import Layout, with_layout_constraint
 from jax.sharding import PartitionSpec as P
 
 HEADS = 16
@@ -50,6 +51,10 @@
 def shift(array, axis, step):
     count = lax.axis_size(axis)
     return lax.ppermute(array, axis, [(i, (i + step) % count) for i in range(count)])
+
+
+def row_major(array):
+    return with_layout_constraint(array, Layout(major_to_minor=tuple(range(array.ndim))))
 
 
 def take_rows(array, start, rows):
@@ -95,25 +100,16 @@
         ],
         axis=1,
     )
-    dense = lax.all_gather(
-        jnp.concatenate([w_query, w_key, w_value, w_out, tail], axis=1),
-        ("dp", "expert"),
-        axis=0,
-        tiled=True,
-    )
+    dense_shard = jnp.concatenate([w_query, w_key, w_value, w_out, tail], axis=1)
+    dense_near = jnp.stack(
+        [dense_shard] + [shift(dense_shard, "expert", -r) for r in range(1, owners)]
+    )
+    dense_near = jnp.roll(dense_near, me, axis=0).reshape(owners * shard, -1)
     q_end = HEADS * HEAD_DIM
     k_end = q_end + KV_HEADS * HEAD_DIM
     v_end = k_end + KV_HEADS * HEAD_DIM
     o_end = v_end + w_out.shape[1]
-    qkv_w = dense[:, :v_end]
-    out_w = dense[:, v_end:o_end]
-    router_w = dense[:, o_end : o_end + EXPERTS]
-    gain_one = dense[:, o_end + EXPERTS]
-    gain_two = dense[:, o_end + EXPERTS + 1]
     down_shard = jnp.swapaxes(w_down, 1, 2)
-    gate_w = lax.all_gather(w_gate, "dp", axis=1, tiled=True)
-    up_w = lax.all_gather(w_up, "dp", axis=1, tiled=True)
-    down_w = lax.all_gather(down_shard, "dp", axis=1, tiled=True)
     early = jnp.concatenate(
         [
             out_grad,
@@ -122,7 +118,22 @@
         ],
         axis=1,
     )
-    early_all = jnp.stack([early] + [shift(early, "expert", r) for r in range(1, owners)])
+    early, dense_near, w_gate, w_up, down_shard = lax.optimization_barrier(
+        (early, dense_near, w_gate, w_up, down_shard)
+    )
+    dense = row_major(lax.all_gather(row_major(dense_near), "dp", axis=0, tiled=True))
+    early = row_major(early)
+    gate_w = lax.all_gather(w_gate, "dp", axis=1, tiled=True)
+    up_w = lax.all_gather(w_up, "dp", axis=1, tiled=True)
+    down_w = lax.all_gather(down_shard, "dp", axis=1, tiled=True)
+    qkv_w = dense[:, :v_end]
+    out_w = dense[:, v_end:o_end]
+    router_w = dense[:, o_end : o_end + EXPERTS]
+    gain_one = dense[:, o_end + EXPERTS]
+    gain_two = dense[:, o_end + EXPERTS + 1]
+    early_all = row_major(
+        jnp.stack([early] + [shift(early, "expert", r) for r in range(1, owners)])
+    )
     inputs = hidden_in.astype(jnp.float32)
     length = inputs.shape[0]
     width = inputs.shape[1]
@@ -192,9 +203,6 @@
     hidden = (activated * up_pre).astype(jnp.bfloat16)
     arrived = (gate_slot[..., None] * grad_rows.astype(jnp.float32)).astype(jnp.bfloat16)
     down_grad = jnp.einsum("sjcd,sjcf->jdf", arrived, hidden, preferred_element_type=jnp.float32)
-    down_total = lax.psum_scatter(
-        down_grad.astype(jnp.bfloat16), "dp", scatter_dimension=1, tiled=True
-    )
     result = jnp.einsum(
         "sjcf,jdf->sjcd", hidden, down_w, preferred_element_type=jnp.float32
     ).astype(jnp.bfloat16)
@@ -203,14 +211,11 @@
     mixed_parts = jnp.einsum("sjct,sjcd->std", picks, weighted, preferred_element_type=jnp.float32)
     slot_grads = jnp.sum(grad_rows.astype(jnp.float32) * result_float, axis=-1)
     gate_grad_parts = jnp.sum(jnp.where(places, slot_grads[..., None], 0.0), axis=2)
-    mixed = mixed_parts[0]
+    mixed = middle + mixed_parts[0]
+    mixed_away = mixed_parts[1:].astype(jnp.bfloat16)
     gate_pieces = [gate_grad_parts[0]]
     for r in range(1, owners):
-        mixed = mixed + shift(mixed_parts[r].astype(jnp.bfloat16), "expert", -r).astype(
-            jnp.float32
-        )
         gate_pieces.append(shift(gate_grad_parts[r], "expert", -r))
-    layer_out = (middle + mixed).astype(jnp.bfloat16)
     gate_grads = jnp.roll(jnp.stack(gate_pieces), me, axis=0).reshape(EXPERTS, length).T
     upstream = out_grad.astype(jnp.float32)
     logit_grads = gates * (gate_grads - jnp.sum(gates * gate_grads, axis=-1, keepdims=True))
@@ -224,6 +229,14 @@
         hidden_grad * up_pre * sigmoid_gate * (1.0 + gate_pre * (1.0 - sigmoid_gate))
     ).astype(jnp.bfloat16)
     up_pre_grad = (hidden_grad * activated).astype(jnp.bfloat16)
+    down_grad = down_grad.astype(jnp.bfloat16)
+    gate_grad = jnp.einsum(
+        "sjcd,sjcf->jdf", rows, gate_pre_grad, preferred_element_type=jnp.float32
+    ).astype(jnp.bfloat16)
+    gate_pre_grad, up_pre_grad, down_grad = lax.optimization_barrier(
+        (gate_pre_grad, up_pre_grad, down_grad)
+    )
+    down_total = lax.psum_scatter(down_grad, "dp", scatter_dimension=1, tiled=True)
     row_grads = jnp.einsum(
         "sjcf,jdf->sjcd", gate_pre_grad, gate_w, preferred_element_type=jnp.float32
     )
@@ -232,22 +245,22 @@
         + jnp.einsum("sjcf,jdf->sjcd", up_pre_grad, up_w, preferred_element_type=jnp.float32)
     ).astype(jnp.bfloat16)
     back_parts = jnp.einsum("sjct,sjcd->std", picks, row_grads, preferred_element_type=jnp.float32)
-    gate_grad = jnp.einsum(
-        "sjcd,sjcf->jdf", rows, gate_pre_grad, preferred_element_type=jnp.float32
-    )
     up_grad = jnp.einsum("sjcd,sjcf->jdf", rows, up_pre_grad, preferred_element_type=jnp.float32)
     gate_total = lax.psum_scatter(
-        gate_grad.astype(jnp.bfloat16), "dp", scatter_dimension=1, tiled=True
-    ).astype(jnp.float32)
+        gate_grad, "dp", scatter_dimension=1, tiled=True
+    )
     up_total = lax.psum_scatter(
         up_grad.astype(jnp.bfloat16), "dp", scatter_dimension=1, tiled=True
-    ).astype(jnp.float32)
-    down_total = jnp.swapaxes(down_total.astype(jnp.float32), 1, 2)
+    )
     normed_grad = normed_grad + back_parts[0]
     for r in range(1, owners):
         normed_grad = normed_grad + shift(
             back_parts[r].astype(jnp.bfloat16), "expert", -r
         ).astype(jnp.float32)
+    normed_grad, mixed_away, down_total = lax.optimization_barrier(
+        (normed_grad, mixed_away, down_total)
+    )
+    mixed_home = [shift(mixed_away[r - 1], "expert", -r) for r in range(1, owners)]
     gain_two_grad = jnp.sum(normed_grad * scaled_two, axis=0)
     scaled_grad = normed_grad * gain_float
     middle_grad = upstream + factor_two * (
@@ -324,6 +337,12 @@
         ],
         axis=1,
     )
+    dense_grad, gate_total, up_total, mixed_home = lax.optimization_barrier(
+        (dense_grad, gate_total, up_total, mixed_home)
+    )
+    for piece in mixed_home:
+        mixed = mixed + piece.astype(jnp.float32)
+    layer_out = mixed.astype(jnp.bfloat16)
     dense_part = lax.psum_scatter(dense_grad, "dp", scatter_dimension=0, tiled=True)
     total = take_rows(dense_part, me * shard, shard).astype(jnp.float32)
     for r in range(1, owners):
@@ -339,9 +358,9 @@
         total[:, v_end:o_end],
         total[:, o_end + EXPERTS + 1],
         total[:, o_end : o_end + EXPERTS],
-        gate_total,
-        up_total,
-        down_total,
+        gate_total.astype(jnp.float32),
+        up_total.astype(jnp.float32),
+        jnp.swapaxes(down_total.astype(jnp.float32), 1, 2),
     )
 
 

time: 948 us -> 721 us (0.76)
  waiting for transfers between devices: 504 us -> 308 us
  starting transfers between devices: 80.4 us -> 30.1 us
  local copies, waits for them, and re-layouts: 43.9 us -> 59.8 us
    reduce_scatter x2, waiting for transfers between devices: 124 us -> 0.01 us  [the longest x1 0.01 us: local(): lax.psum_scatter(down_grad, 'dp', scatter_dimension=1, tiled=True)]
    all_gather x1, waiting for transfers between devices: 128 us -> 39.4 us  [local(): lax.all_gather(row_major(dense_near), 'dp', axis=0, tiled=True)]
    reduce_scatter x1, waiting for transfers between devices: 72.3 us -> 0.01 us  [local(): lax.psum_scatter(up_grad.astype(jnp.bfloat16), 'dp', scatter_dimension=1,...]
    ppermute x18 -> x21, waiting for transfers between devices: 151 us -> 208 us  [shift(): lax.ppermute(array, axis, [(i, (i + step) % count) for i in range(count)])]
    ppermute x18 -> x21, starting transfers between devices: 80 us -> 29.8 us  [shift(): lax.ppermute(array, axis, [(i, (i + step) % count) for i in range(count)])]
    reduce_scatter x1, waiting for transfers between devices: 17.7 us -> 58.1 us  [local(): lax.psum_scatter(dense_grad, 'dp', scatter_dimension=0, tiled=True)]
  transfers between devices with their start and end apart: 26 -> 29, of which waited for: 12 -> 9; matrix products, arithmetic and copies ran while one was open for 23% -> 41% of each run, Pallas kernels for 0% -> 0%
where the time goes in v2:
time: 721 us; the launch traced here: 717 us
  waiting for transfers between devices  308 us (43%)
  matrix products  250 us (35%)
  local copies, waits for them, and re-layouts  59.8 us (8%)
  other arithmetic  53.7 us (7%)
  starting transfers between devices  30.1 us (4%)
  between operations  15.3 us (2%)
    ppermute x21, waiting for transfers between devices, shift(): lax.ppermute(array, axis, [(i, (i + step) % count) for i in range(count)])  208 us
    reduce_scatter x1, waiting for transfers between devices, local(): lax.psum_scatter(dense_grad, 'dp', scatter_dimension=0, tiled=True)  58.1 us
    all_gather x1, waiting for transfers between devices, local(): lax.all_gather(row_major(dense_near), 'dp', axis=0, tiled=True)  39.4 us
    ppermute x21, starting transfers between devices, shift(): lax.ppermute(array, axis, [(i, (i + step) % count) for i in range(count)])  29.8 us
    dot_general x1, matrix products, local(): jnp.einsum('sjct,sjcd->std', picks, row_grads, preferred_element_type=jnp...  22.3 us
    dot_general x1, matrix products, local(): jnp.einsum('sjcd,jdf->sjcf', arrived, down_w, preferred_element_type=jnp....  18.1 us
    dot_general x1, matrix products, local(): jnp.einsum('sjcd,jdf->sjcf', rows, up_w, preferred_element_type=jnp.float32)  15.3 us
    dot_general x1, matrix products, local(): jnp.einsum('qgrd,kgd->grqk', attended_grad, values_in, preferred_element_...  14.7 us
  transfers between devices with their start and end apart: 29, of which 9 were waited for; matrix products, arithmetic and copies ran while one was open for 41% of the time, Pallas kernels for 0%

profile of v2, /device:TPU:0, one launch (start us, length us, event | category | flops | bytes accessed | tf_op | source)
XLA Modules:
  0.0 716.9 jit_solution(3672820280420939904)
XLA Ops:
  9.7 5.1 collective-permute-start
  22.2 10.0 %collective-permute-done.1 = bf16[32,3200]{1,0:T(8,128)(2,1)S(1)} collective-permute-done((bf16[32,3200]{1,0:T(8,128)(2,1)S(1)}, bf16[32,3200]{1,0:T(8,128)(2,1)S(1)}, u32[]{:S(2)}, u32[]{:S(2)}) %collective-permute-start.1) | collective-permute-done | bytes 204832 | tf_op jit(solution)/shard_map/ppermute | solution.py:53
  41.2 39.4 %all-gather.5.cloned.1.call-done = bf16[1024,3200]{1,0:T(8,128)(2,1)} async-done(((bf16[128,3200]{1,0:T(8,128)(2,1)}), bf16[1024,3200]{1,0:T(8,128)(2,1)}) %all-gather.5.cloned.1.call-update) | async-done | bytes 6553616 | tf_op jit(solution)/shard_map/all_gather | solution.py:124
  96.2 7.3 %fusion.157 = (f32[8,2,512]{2,1,0:T(2,128)S(1)}, f32[8,2,512,512]{2,3,1,0:T(8,128)}) fusion(bf16[512,8,2,32]{0,3,2,1:T(8,128)(2,1)S(1)} %bitcast.300, bf16[512,8,2,32]{0,3,2,1:T(8,128)(2,1)S(1)} %bitcast.298, bf16[512,8,32]{0,2,1:T(8,128)(2,1)S(1)} %get-tuple-element.171, bf16[512,8,32]{0,2,1:T(8,128)(2,1)S(1)} %get-tuple-element.170, ...), kind=kOutput, calls=%fused_computation.229 | convolution fusion | flops 552591360 | bytes 18644992 | tf_op jit(solution)/shard_map/qgrd,kgd->grqk/dot_general | solution.py:66
  103.6 8.2 %exponential_reduce_fusion = f32[8,2,512]{2,1,0:T(2,128)S(1)} fusion(f32[8,2,512,512]{2,3,1,0:T(8,128)} %get-tuple-element.186, f32[8,2,512]{2,1,0:T(2,128)S(1)} %get-tuple-element.185), kind=kLoop, calls=%fused_computation.18 | loop fusion | flops 8380416 | bytes 16842752 | tf_op jit(solution)/shard_map/reduce_sum | solution.py:161
  111.8 8.6 %fusion.116 = bf16[8,64,2,512]{3,1,2,0:T(8,128)(2,1)S(1)} fusion(bf16[512,8,64,1]{0,2,3,1:T(8,128)(2,1)S(1)} %bitcast.293, f32[8,2,512,512]{2,3,1,0:T(8,128)} %get-tuple-element.186, f32[8,2,512]{2,1,0:T(2,128)S(1)} %bitcast.306), kind=kOutput, calls=%fused_computation.128 | convolution fusion | flops 545783808 | bytes 18382848 | tf_op jit(solution)/shard_map/grqk,kgd->qgrd/dot_general | solution.py:163
  129.1 13.0 %collective-permute-done.4 = bf16[512,1152]{1,0:T(8,128)(2,1)} collective-permute-done((bf16[512,1152]{1,0:T(8,128)(2,1)}, bf16[512,1152]{1,0:T(8,128)(2,1)}, u32[]{:S(2)}, u32[]{:S(2)}) %collective-permute-start.4) | collective-permute-done | bytes 1179680 | tf_op jit(solution)/shard_map/ppermute | solution.py:53
  148.5 14.5 %collective-permute-done.8 = bf16[512,1024]{1,0:T(8,128)(2,1)} collective-permute-done((bf16[512,1024]{1,0:T(8,128)(2,1)S(1)}, bf16[512,1024]{1,0:T(8,128)(2,1)}, u32[]{:S(2)}, u32[]{:S(2)}) %collective-permute-start.8) | collective-permute-done | bytes 1048608 | tf_op jit(solution)/shard_map/ppermute | solution.py:53
  163.0 67.5 %collective-permute-done.7 = bf16[512,1024]{1,0:T(8,128)(2,1)} collective-permute-done((bf16[512,1024]{1,0:T(8,128)(2,1)S(1)}, bf16[512,1024]{1,0:T(8,128)(2,1)}, u32[]{:S(2)}, u32[]{:S(2)}) %collective-permute-start.7) | collective-permute-done | bytes 1048608 | tf_op jit(solution)/shard_map/ppermute | solution.py:53
  236.8 9.5 %fusion.54 = bf16[4,8,152,1024]{3,2,1,0:T(8,128)(2,1)} fusion(s32[4,8,512]{2,1,0:T(8,128)S(1)} %copy.176, bf16[1,512,1024]{2,1,0:T(8,128)(2,1)} %bitcast.29, bf16[1,512,1024]{2,1,0:T(8,128)(2,1)} %bitcast.28, bf16[1,512,1024]{2,1,0:T(8,128)(2,1)} %bitcast.27, bf16[1,512,1024]{2,1,0:T(8,128)(2,1)S(1)} %copy-done.25), kind=kOutput, calls=%fused_computation.63 | convolution fusion | flops 5114036224 | bytes 14221312 | tf_op jit(solution)/shard_map/sjct,std->sjcd/dot_general | solution.py:196
  246.3 13.1 %fusion.27 = f32[8,512,4,152]{1,3,2,0:T(8,128)} fusion(bf16[4,8,152,1024]{3,2,1,0:T(8,128)(2,1)} %fusion.54, bf16[8,1024,512]{2,1,0:T(8,128)(2,1)} %all-gather.9.cloned.1.call-done), kind=kOutput, calls=%fused_computation.47 | convolution fusion | flops 5100273664 | bytes 28311552 | tf_op jit(solution)/shard_map/sjcd,jdf->sjcf/dot_general | solution.py:199
  259.4 15.3 %fusion.15 = (bf16[4,8,152,512]{3,2,0,1:T(8,128)(2,1)}, f32[8,512,4,152]{1,3,2,0:T(8,128)}) fusion(f32[8,512,4,152]{1,3,2,0:T(8,128)} %fusion.27, bf16[4,8,152,1024]{3,2,1,0:T(8,128)(2,1)} %fusion.54, bf16[8,1024,512]{2,1,0:T(8,128)(2,1)} %all-gather.11.cloned.1.call-done), kind=kOutput, calls=%fused_computation.29 | convolution fusion | flops 5115215872 | bytes 43253760 | tf_op jit(solution)/shard_map/sjcd,jdf->sjcf/dot_general | solution.py:200
  274.7 11.9 %fusion.48 = bf16[8,1024,4,152]{1,3,2,0:T(8,128)(2,1)} fusion(bf16[4,8,152,512]{3,2,0,1:T(8,128)(2,1)} %get-tuple-element.189, bf16[8,1024,512]{2,1,0:T(8,128)(2,1)} %all-gather.7.cloned.1.call-done), kind=kOutput, calls=%fused_computation.60 | convolution fusion | flops 5105254400 | bytes 23330816 | tf_op jit(solution)/shard_map/sjcf,jdf->sjcd/dot_general | solution.py:206
  286.6 12.2 %fusion.1 = (f32[4,8,152]{2,0,1:T(4,128)S(1)}, bf16[4,8,152,1024]{3,2,0,1:T(8,128)(2,1)}) fusion(bf16[8,1024,4,152]{1,3,2,0:T(8,128)(2,1)} %fusion.48, bf16[1,512,1152]{2,1,0:T(8,128)(2,1)} %bitcast.23, bf16[1,512,1152]{2,1,0:T(8,128)(2,1)} %bitcast.22, bf16[1,512,1152]{2,1,0:T(8,128)(2,1)} %bitcast.21, bf16[1,512,1152]{2,1,0:T(8,128)(2,1)} %bitcast.20, ...), kind=kOutput, calls=%fused_computation.3 | convolution fusion | flops 5144439808 | bytes 24726528 | tf_op jit(solution)/shard_map/sjct,std->sjcd/dot_general | solution.py:193
  302.8 11.6 %bitcast_convert_fusion.2 = bf16[8,1024,512]{2,1,0:T(8,128)(2,1)} fusion(bf16[4,8,152,512]{3,2,0,1:T(8,128)(2,1)S(1)} %copy-done.44, bf16[4,8,152,1024]{3,2,0,1:T(8,128)(2,1)} %get-tuple-element.192, f32[4,8,152]{2,0,1:T(4,128)S(1)} %copy.180), kind=kOutput, calls=%fused_computation.15 | convolution fusion | flops 5119410176 | bytes 23350272 | tf_op jit(solution)/shard_map/sjcd,sjcf->jdf/dot_general | solution.py:205
  314.4 18.1 %fusion.14 = (bf16[4,8,152,512]{3,2,0,1:T(8,128)(2,1)}, bf16[4,8,152,512]{3,2,0,1:T(8,128)(2,1)}) fusion(f32[8,512,4,152]{1,3,2,0:T(8,128)} %fusion.27, f32[8,512,4,152]{1,3,2,0:T(8,128)} %get-tuple-element.190, bf16[4,8,152,1024]{3,2,0,1:T(8,128)(2,1)} %get-tuple-element.192, f32[4,8,152]{2,0,1:T(4,128)S(1)} %copy.180, ...), kind=kOutput, calls=%fused_computation.27 | convolution fusion | flops 5147590656 | bytes 48253952 | tf_op jit(solution)/shard_map/sjcd,jdf->sjcf/dot_general | solution.py:227
  332.6 13.8 %bitcast_convert_fusion.1 = bf16[8,1024,512]{2,1,0:T(8,128)(2,1)} fusion(bf16[4,8,152,1024]{3,2,1,0:T(8,128)(2,1)} %fusion.54, bf16[4,8,152,512]{3,2,0,1:T(8,128)(2,1)} %get-tuple-element.74), kind=kOutput, calls=%fused_computation.9 | convolution fusion | flops 5104467968 | bytes 23330816 | tf_op jit(solution)/shard_map/sjcd,sjcf->jdf/dot_general | solution.py:233
  346.6 13.1 %bitcast_convert_fusion = bf16[8,1024,512]{2,1,0:T(8,128)(2,1)} fusion(bf16[4,8,152,1024]{3,2,1,0:T(8,128)(2,1)} %fusion.54, bf16[4,8,152,512]{3,2,0,1:T(8,128)(2,1)} %get-tuple-element.75), kind=kOutput, calls=%fused_computation.8 | convolution fusion | flops 5104467968 | bytes 23330816 | tf_op jit(solution)/shard_map/sjcd,sjcf->jdf/dot_general | solution.py:248
  359.6 10.6 %fusion.71 = f32[4,512,1024]{2,1,0:T(8,128)} fusion(s32[4,8,512]{2,1,0:T(8,128)S(1)} %copy.176, bf16[8,1024,4,152]{1,3,2,0:T(8,128)(2,1)} %fusion.48, f32[4,8,152]{2,0,1:T(4,128)S(1)} %copy.180), kind=kOutput, calls=%fused_computation.83 | convolution fusion | flops 5117706240 | bytes 18435072 | tf_op jit(solution)/shard_map/sjct,sjcd->std/dot_general | solution.py:211
  370.3 13.8 %fusion.38 = f32[8,1024,4,152]{1,3,0,2:T(8,128)} fusion(bf16[8,1024,512]{2,1,0:T(8,128)(2,1)} %all-gather.11.cloned.1.call-done, bf16[4,8,152,512]{3,2,0,1:T(8,128)(2,1)} %get-tuple-element.75), kind=kOutput, calls=%fused_computation.56 | convolution fusion | flops 5100273664 | bytes 33292288 | tf_op jit(solution)/shard_map/sjcf,jdf->sjcd/dot_general | solution.py:245
  384.1 22.3 %fusion.159 = (bf16[4,512,1024]{2,1,0:T(8,128)(2,1)}, f32[4,512,1024]{2,1,0:T(8,128)}) fusion(f32[8,1024,4,152]{1,3,0,2:T(8,128)} %fusion.38, bf16[8,1024,512]{2,1,0:T(8,128)(2,1)} %all-gather.9.cloned.1.call-done, bf16[4,8,152,512]{3,2,0,1:T(8,128)(2,1)} %get-tuple-element.74, s32[4,8,512]{2,1,0:T(8,128)S(1)} %copy.176), kind=kOutput, calls=%fused_computation.231 | convolution fusion | flops 10215096320 | bytes 45940736 | tf_op jit(solution)/shard_map/sjct,sjcd->std/dot_general | solution.py:247
  415.8 6.1 slice.309
  423.1 80.6 %collective-permute-done.10 = f32[8,512]{1,0:T(8,128)S(1)} collective-permute-done((f32[8,512]{1,0:T(8,128)S(1)}, f32[8,512]{1,0:T(8,128)S(1)}, u32[]{:S(2)}, u32[]{:S(2)}) %collective-permute-start.10) | collective-permute-done | bytes 16416 | tf_op jit(solution)/shard_map/ppermute | solution.py:53
  531.0 14.7 %fusion.4 = (f32[8,2,512]{2,1,0:T(2,128)}, f32[8,512,512,2]{2,1,3,0:T(8,128)}) fusion(f32[8,2,512,512]{2,3,1,0:T(8,128)} %get-tuple-element.186, f32[8,2,512]{2,1,0:T(2,128)} %bitcast.307, bf16[512,8,64,1]{0,2,3,1:T(8,128)(2,1)S(1)} %bitcast.294, bf16[512,8,2,64]{0,3,2,1:T(8,128)(2,1)} %bitcast.289), kind=kOutput, calls=%fused_computation.12 | convolution fusion | flops 549445632 | bytes 35192832 | tf_op jit(solution)/shard_map/qgrd,kgd->grqk/dot_general | solution.py:290
  548.3 11.1 %fusion.6 = bf16[8,2,512,512]{2,3,1,0:T(8,128)(2,1)} fusion(f32[8,512,512,2]{2,1,3,0:T(8,128)} %get-tuple-element.198, f32[8,2,512,512]{2,3,1,0:T(8,128)S(1)} %bitcast.288, f32[8,2,512]{2,1,0:T(2,128)} %get-tuple-element.197, f32[8,2,512]{2,1,0:T(2,128)} %bitcast.308), kind=kLoop, calls=%fused_computation.14 | loop fusion | flops 16777216 | bytes 42008576 | tf_op jit(solution)/shard_map/convert_element_type | solution.py:294
  559.4 6.1 fusion.124
  577.8 7.3 %fusion.91 = (f32[512]{0:T(512)S(1)}, bf16[1024]{0:T(1024)(128)(2,1)S(1)}, f32[512,1024]{1,0:T(8,128)}) fusion(bf16[512,1024]{1,0:T(8,128)(2,1)} %param.21, f32[1024]{0:T(1024)S(1)} %copy-done.41, f32[512]{0:T(512)S(1)} %copy-done.43, bf16[1024,3200]{1,0:T(8,128)(2,1)} %all-gather.5.cloned.1.call-done, bf16[512,512]{0,1:T(8,128)(2,1)} %bitcast.310, ...), kind=kOutput, calls=%fused_computation.96 | convolution fusion | flops 2157443584 | bytes 9447424 | tf_op jit(solution)/shard_map/tk,dk->td/dot_general | solution.py:316
  593.0 10.8 %concatenate.61 = bf16[1024,3200]{1,0:T(8,128)(2,1)} concatenate(bf16[1024,2048]{1,0:T(8,128)(2,1)} %convolution_convert_fusion, bf16[1024,1024]{1,0:T(8,128)(2,1)} %convolution_convert_fusion.1, bf16[1024,32]{1,0:T(8,128)(2,1)S(1)} %copy-done.24, bf16[1024,1]{1,0:T(8,128)(2,1)S(1)} %broadcast_in_dim.115, bf16[1024,1]{1,0:T(8,128)(2,1)S(1)} %broadcast_in_dim.116, ...), dimensions={1} | concatenate | bytes 13107200 | tf_op jit(solution)/shard_map/concatenate | solution.py:332
  603.8 16.2 %collective-permute-done.16 = bf16[512,1024]{1,0:T(8,128)(2,1)} collective-permute-done((bf16[512,1024]{1,0:T(8,128)(2,1)}, bf16[512,1024]{1,0:T(8,128)(2,1)}, u32[]{:S(2)}, u32[]{:S(2)}) %collective-permute-start.16) | collective-permute-done | bytes 1048608 | tf_op jit(solution)/shard_map/ppermute | solution.py:53
  625.9 58.1 %reduce-scatter.11.cloned.1.call-done = bf16[128,3200]{1,0:T(8,128)(2,1)} async-done(((bf16[1024,3200]{1,0:T(8,128)(2,1)}), bf16[128,3200]{1,0:T(8,128)(2,1)}) %reduce-scatter.11.cloned.1.call-update) | async-done | bytes 819216 | tf_op jit(solution)/shard_map/reduce_scatter | solution.py:346
  689.7 6.7 fusion.95
  699.5 6.6 collective-permute-done.19
  (247 shorter events, 138.6 us)
Async XLA Ops:
  7.2 73.4 %all-gather.5.cloned.1.call-start = ((), (), s32[]{:S(2)}) async-start(), calls=%async_computation.4 | async-start | bytes 7372800 | tf_op jit(solution)/shard_map/all_gather | solution.py:124
  9.7 12.5 %collective-permute-start = (bf16[32,3200]{1,0:T(8,128)(2,1)S(1)}, bf16[32,3200]{1,0:T(8,128)(2,1)S(1)}, u32[]{:S(2)}, u32[]{:S(2)}) collective-permute-start(bf16[32,3200]{1,0:T(8,128)(2,1)S(1)} %concatenate.51), channel_id=1, source_target_pairs={{0,3},{1,0},{2,1},{3,2},{4,7},{5,4},{6,5},{7,6},{8,11},{9,8},{10,9... | collective-permute-start | bytes 614408 | tf_op jit(solution)/shard_map/ppermute | solution.py:53
  14.8 17.4 %collective-permute-start.1 = (bf16[32,3200]{1,0:T(8,128)(2,1)S(1)}, bf16[32,3200]{1,0:T(8,128)(2,1)S(1)}, u32[]{:S(2)}, u32[]{:S(2)}) collective-permute-start(bf16[32,3200]{1,0:T(8,128)(2,1)S(1)} %concatenate.51), channel_id=1, source_target_pairs={{0,2},{1,3},{2,0},{3,1},{4,6},{5,7},{6,4},{7,5},{8,10},{9,11},{10,... | collective-permute-start | bytes 614408 | tf_op jit(solution)/shard_map/ppermute | solution.py:53
  14.8 17.4 %collective-permute-start.2 = (bf16[32,3200]{1,0:T(8,128)(2,1)S(1)}, bf16[32,3200]{1,0:T(8,128)(2,1)S(1)}, u32[]{:S(2)}, u32[]{:S(2)}) collective-permute-start(bf16[32,3200]{1,0:T(8,128)(2,1)S(1)} %concatenate.51), channel_id=1, source_target_pairs={{0,1},{1,2},{2,3},{3,0},{4,5},{5,6},{6,7},{7,4},{8,9},{9,10},{10,1... | collective-permute-start | bytes 614408 | tf_op jit(solution)/shard_map/ppermute | solution.py:53
  33.4 212.9 %all-gather.9.cloned.1.call-start = ((), (), s32[]{:S(2)}) async-start(), calls=%async_computation.6 | async-start | bytes 9437184 | tf_op jit(solution)/shard_map/all_gather | solution.py:126
  34.1 225.3 %all-gather.11.cloned.1.call-start = ((), (), s32[]{:S(2)}) async-start(), calls=%async_computation.7 | async-start | bytes 9437184 | tf_op jit(solution)/shard_map/all_gather | solution.py:127
  34.8 239.8 %all-gather.7.cloned.1.call-start = ((), (), s32[]{:S(2)}) async-start(), calls=%async_computation.5 | async-start | bytes 9437184 | tf_op jit(solution)/shard_map/all_gather | solution.py:128
  35.4 477.9 %reduce-scatter.5.cloned.1.call-start = ((), (), s32[]{:S(2)}) async-start(), calls=%async_computation.8 | async-start | bytes 9437184 | tf_op jit(solution)/shard_map/reduce_scatter | solution.py:239
  36.2 59.6 %copy-start.16 = (f32[512,32]{0,1:T(8,128)}, f32[512,32]{0,1:T(8,128)S(1)}, u32[]{:S(2)}) copy-start(f32[512,32]{0,1:T(8,128)S(1)} %get-tuple-element.183) | copy-start | bytes 196612
  36.2 59.6 %copy-start.18 = (f32[512,32]{0,1:T(8,128)}, f32[512,32]{0,1:T(8,128)S(1)}, u32[]{:S(2)}) copy-start(f32[512,32]{0,1:T(8,128)S(1)} %get-tuple-element.184) | copy-start | bytes 196612
  36.2 91.4 %collective-permute-start.5 = (bf16[512,1152]{1,0:T(8,128)(2,1)}, bf16[512,1152]{1,0:T(8,128)(2,1)}, u32[]{:S(2)}, u32[]{:S(2)}) collective-permute-start(bf16[512,1152]{1,0:T(8,128)(2,1)} %concatenate.50), channel_id=1, source_target_pairs={{0,3},{1,0},{2,1},{3,2},{4,7},{5,4},{6,5},{7,6},{8,11},{9,8},{10,9... | collective-permute-start | bytes 3538952 | tf_op jit(solution)/shard_map/ppermute | solution.py:53
  36.5 105.7 %collective-permute-start.4 = (bf16[512,1152]{1,0:T(8,128)(2,1)}, bf16[512,1152]{1,0:T(8,128)(2,1)}, u32[]{:S(2)}, u32[]{:S(2)}) collective-permute-start(bf16[512,1152]{1,0:T(8,128)(2,1)} %concatenate.50), channel_id=1, source_target_pairs={{0,2},{1,3},{2,0},{3,1},{4,6},{5,7},{6,4},{7,5},{8,10},{9,11},{10,... | collective-permute-start | bytes 3538952 | tf_op jit(solution)/shard_map/ppermute | solution.py:53
  39.1 103.0 %collective-permute-start.3 = (bf16[512,1152]{1,0:T(8,128)(2,1)}, bf16[512,1152]{1,0:T(8,128)(2,1)}, u32[]{:S(2)}, u32[]{:S(2)}) collective-permute-start(bf16[512,1152]{1,0:T(8,128)(2,1)} %concatenate.50), channel_id=1, source_target_pairs={{0,1},{1,2},{2,3},{3,0},{4,5},{5,6},{6,7},{7,4},{8,9},{9,10},{10,1... | collective-permute-start | bytes 3538952 | tf_op jit(solution)/shard_map/ppermute | solution.py:53
  82.0 65.2 %copy-start.36 = (f32[1024]{0:T(1024)}, f32[1024]{0:T(1024)S(1)}, u32[]{:S(2)}) copy-start(f32[1024]{0:T(1024)S(1)} %get-tuple-element.146) | copy-start | bytes 12292
  124.0 39.0 %collective-permute-start.8 = (bf16[512,1024]{1,0:T(8,128)(2,1)S(1)}, bf16[512,1024]{1,0:T(8,128)(2,1)}, u32[]{:S(2)}, u32[]{:S(2)}) collective-permute-start(bf16[512,1024]{1,0:T(8,128)(2,1)S(1)} %multiply_convert_fusion), channel_id=1, source_target_pairs={{0,3},{1,0},{2,1},{3,2},{4,7},{5,4},{6,5},{7,6},{8,11},{9,8},{10,9... | collective-permute-start | bytes 3145736 | tf_op jit(solution)/shard_map/ppermute | solution.py:53
  127.6 102.9 %collective-permute-start.7 = (bf16[512,1024]{1,0:T(8,128)(2,1)S(1)}, bf16[512,1024]{1,0:T(8,128)(2,1)}, u32[]{:S(2)}, u32[]{:S(2)}) collective-permute-start(bf16[512,1024]{1,0:T(8,128)(2,1)S(1)} %multiply_convert_fusion), channel_id=1, source_target_pairs={{0,2},{1,3},{2,0},{3,1},{4,6},{5,7},{6,4},{7,5},{8,10},{9,11},{10,... | collective-permute-start | bytes 3145736 | tf_op jit(solution)/shard_map/ppermute | solution.py:53
  127.6 102.9 %collective-permute-start.6 = (bf16[512,1024]{1,0:T(8,128)(2,1)S(1)}, bf16[512,1024]{1,0:T(8,128)(2,1)}, u32[]{:S(2)}, u32[]{:S(2)}) collective-permute-start(bf16[512,1024]{1,0:T(8,128)(2,1)S(1)} %multiply_convert_fusion), channel_id=1, source_target_pairs={{0,1},{1,2},{2,3},{3,0},{4,5},{5,6},{6,7},{7,4},{8,9},{9,10},{10,1... | collective-permute-start | bytes 3145736 | tf_op jit(solution)/shard_map/ppermute | solution.py:53
  332.5 271.2 %reduce-scatter.7.cloned.1.call-start = ((), (), s32[]{:S(2)}) async-start(), calls=%async_computation.9 | async-start | bytes 9437184 | tf_op jit(solution)/shard_map/reduce_scatter | solution.py:249
  346.5 257.3 %reduce-scatter.9.cloned.1.call-start = ((), (), s32[]{:S(2)}) async-start(), calls=%async_computation.10 | async-start | bytes 9437184 | tf_op jit(solution)/shard_map/reduce_scatter | solution.py:252
  346.5 75.4 %collective-permute-start.9 = (f32[8,512]{1,0:T(8,128)S(1)}, f32[8,512]{1,0:T(8,128)S(1)}, u32[]{:S(2)}, u32[]{:S(2)}) collective-permute-start(f32[8,512]{1,0:T(8,128)S(1)} %get-tuple-element.182), channel_id=1, source_target_pairs={{0,3},{1,0},{2,1},{3,2},{4,7},{5,4},{6,5},{7,6},{8,11},{9,8},{10,9... | collective-permute-start | bytes 49160 | tf_op jit(solution)/shard_map/ppermute | solution.py:53
  370.3 313.7 %reduce-scatter.11.cloned.1.call-start = ((), (), s32[]{:S(2)}) async-start(), calls=%async_computation.11 | async-start | bytes 7372800 | tf_op jit(solution)/shard_map/reduce_scatter | solution.py:346
  410.0 98.8 %collective-permute-start.14 = (bf16[512,1024]{1,0:T(8,128)(2,1)}, bf16[512,1024]{1,0:T(8,128)(2,1)}, u32[]{:S(2)}, u32[]{:S(2)}) collective-permute-start(bf16[512,1024]{1,0:T(8,128)(2,1)} %get-tuple-element.159), channel_id=1, source_target_pairs={{0,1},{1,2},{2,3},{3,0},{4,5},{5,6},{6,7},{7,4},{8,9},{9,10},{10,1... | collective-permute-start | bytes 3145736 | tf_op jit(solution)/shard_map/ppermute | solution.py:53
  412.0 96.7 %collective-permute-start.13 = (bf16[512,1024]{1,0:T(8,128)(2,1)}, bf16[512,1024]{1,0:T(8,128)(2,1)}, u32[]{:S(2)}, u32[]{:S(2)}) collective-permute-start(bf16[512,1024]{1,0:T(8,128)(2,1)} %get-tuple-element.160), channel_id=1, source_target_pairs={{0,2},{1,3},{2,0},{3,1},{4,6},{5,7},{6,4},{7,5},{8,10},{9,11},{10,... | collective-permute-start | bytes 3145736 | tf_op jit(solution)/shard_map/ppermute | solution.py:53
  412.0 96.7 %collective-permute-start.12 = (bf16[512,1024]{1,0:T(8,128)(2,1)}, bf16[512,1024]{1,0:T(8,128)(2,1)}, u32[]{:S(2)}, u32[]{:S(2)}) collective-permute-start(bf16[512,1024]{1,0:T(8,128)(2,1)} %get-tuple-element.158), channel_id=1, source_target_pairs={{0,3},{1,0},{2,1},{3,2},{4,7},{5,4},{6,5},{7,6},{8,11},{9,8},{10,9... | collective-permute-start | bytes 3145736 | tf_op jit(solution)/shard_map/ppermute | solution.py:53
  414.4 89.3 %collective-permute-start.10 = (f32[8,512]{1,0:T(8,128)S(1)}, f32[8,512]{1,0:T(8,128)S(1)}, u32[]{:S(2)}, u32[]{:S(2)}) collective-permute-start(f32[8,512]{1,0:T(8,128)S(1)} %get-tuple-element.181), channel_id=1, source_target_pairs={{0,2},{1,3},{2,0},{3,1},{4,6},{5,7},{6,4},{7,5},{8,10},{9,11},{10,... | collective-permute-start | bytes 49160 | tf_op jit(solution)/shard_map/ppermute | solution.py:53
  421.9 81.8 %collective-permute-start.11 = (f32[8,512]{1,0:T(8,128)S(1)}, f32[8,512]{1,0:T(8,128)S(1)}, u32[]{:S(2)}, u32[]{:S(2)}) collective-permute-start(f32[8,512]{1,0:T(8,128)S(1)} %get-tuple-element.179), channel_id=1, source_target_pairs={{0,1},{1,2},{2,3},{3,0},{4,5},{5,6},{6,7},{7,4},{8,9},{9,10},{10,1... | collective-permute-start | bytes 49160 | tf_op jit(solution)/shard_map/ppermute | solution.py:53
  528.9 74.9 %collective-permute-start.15 = (bf16[512,1024]{1,0:T(8,128)(2,1)}, bf16[512,1024]{1,0:T(8,128)(2,1)}, u32[]{:S(2)}, u32[]{:S(2)}) collective-permute-start(bf16[512,1024]{1,0:T(8,128)(2,1)} %get-tuple-element.163), channel_id=1, source_target_pairs={{0,3},{1,0},{2,1},{3,2},{4,7},{5,4},{6,5},{7,6},{8,11},{9,8},{10,9... | collective-permute-start | bytes 3145736 | tf_op jit(solution)/shard_map/ppermute | solution.py:53
  529.5 90.5 %collective-permute-start.16 = (bf16[512,1024]{1,0:T(8,128)(2,1)}, bf16[512,1024]{1,0:T(8,128)(2,1)}, u32[]{:S(2)}, u32[]{:S(2)}) collective-permute-start(bf16[512,1024]{1,0:T(8,128)(2,1)} %get-tuple-element.162), channel_id=1, source_target_pairs={{0,2},{1,3},{2,0},{3,1},{4,6},{5,7},{6,4},{7,5},{8,10},{9,11},{10,... | collective-permute-start | bytes 3145736 | tf_op jit(solution)/shard_map/ppermute | solution.py:53
  529.5 90.5 %collective-permute-start.17 = (bf16[512,1024]{1,0:T(8,128)(2,1)}, bf16[512,1024]{1,0:T(8,128)(2,1)}, u32[]{:S(2)}, u32[]{:S(2)}) collective-permute-start(bf16[512,1024]{1,0:T(8,128)(2,1)} %get-tuple-element.161), channel_id=1, source_target_pairs={{0,1},{1,2},{2,3},{3,0},{4,5},{5,6},{6,7},{7,4},{8,9},{9,10},{10,1... | collective-permute-start | bytes 3145736 | tf_op jit(solution)/shard_map/ppermute | solution.py:53
  685.2 14.4 %collective-permute-start.20 = (bf16[32,3200]{1,0:T(8,128)(2,1)S(1)}, bf16[32,3200]{1,0:T(8,128)(2,1)S(1)}, u32[]{:S(2)}, u32[]{:S(2)}) collective-permute-start(bf16[32,3200]{1,0:T(8,128)(2,1)S(1)} %get-tuple-element.173), channel_id=1, source_target_pairs={{0,3},{1,0},{2,1},{3,2},{4,7},{5,4},{6,5},{7,6},{8,11},{9,8},{10,9... | collective-permute-start | bytes 614408 | tf_op jit(solution)/shard_map/ppermute | solution.py:53
  688.6 17.6 %collective-permute-start.19 = (bf16[32,3200]{1,0:T(8,128)(2,1)S(1)}, bf16[32,3200]{1,0:T(8,128)(2,1)S(1)}, u32[]{:S(2)}, u32[]{:S(2)}) collective-permute-start(bf16[32,3200]{1,0:T(8,128)(2,1)S(1)} %get-tuple-element.174), channel_id=1, source_target_pairs={{0,2},{1,3},{2,0},{3,1},{4,6},{5,7},{6,4},{7,5},{8,10},{9,11},{10,... | collective-permute-start | bytes 614408 | tf_op jit(solution)/shard_map/ppermute | solution.py:53
  688.6 17.6 %collective-permute-start.18 = (bf16[32,3200]{1,0:T(8,128)(2,1)S(1)}, bf16[32,3200]{1,0:T(8,128)(2,1)S(1)}, u32[]{:S(2)}, u32[]{:S(2)}) collective-permute-start(bf16[32,3200]{1,0:T(8,128)(2,1)S(1)} %get-tuple-element.172), channel_id=1, source_target_pairs={{0,1},{1,2},{2,3},{3,0},{4,5},{5,6},{6,7},{7,4},{8,9},{9,10},{10,1... | collective-permute-start | bytes 614408 | tf_op jit(solution)/shard_map/ppermute | solution.py:53
  (46 other events, 438.6 us)
Sparse Core Ops, SparseCore 0:
  33.5 47.0 all-gather.4
  82.5 54.3 all-gather.8
  138.8 54.3 all-gather.10
  195.0 54.3 all-gather.6
  332.7 69.2 reduce-scatter.4
  405.7 71.2 reduce-scatter.6
  480.4 71.2 reduce-scatter.8
  620.2 63.7 reduce-scatter.10
